TPU v7x, 512 devices: a whole 4x4x16 slice. The times are simulated.
512 devices in a mesh: dp: 64 (over z, x), tensor: 8 (over y, core).
Axes of the slice: x: 4, y: 4, z: 16, core: 2. Of those that a mesh axis runs over, the one named last changes fastest.
Arguments:
- decode_input_rows: bfloat16 [8192, 12288], P('dp', 'tensor'), may hold values from -6 to 6
- decode_adapter_index: int32 [8192], P('dp'), may hold values from 0 to 127, as said below
- adapter_storage_index: int32 [128], replicated, may hold values from 0 to 127, as said below
- learner_input_rows: bfloat16 [8192, 12288], P('dp', 'tensor'), may hold values from -6 to 6
- learner_gradient: bfloat16 [8192, 28672], P('dp', 'tensor'), may hold values from -6 to 6
- block_adapter_index: int32 [64], P('dp'), may hold values from 0 to 127, as said below
- block_live_count: int32 [64], P('dp'), may hold values from 16 to 128, as said below
- adapter_down_weight: bfloat16 [128, 64, 12288], P('dp', None, 'tensor'), may hold values from -6 to 6
- adapter_up_weight: bfloat16 [128, 64, 28672], P('dp', None, 'tensor'), may hold values from -6 to 6
Outputs:
- dec_delta: bfloat16 [8192, 28672], P('dp', 'tensor')
- refreshed_down_weight: bfloat16 [128, 64, 12288], P('dp', None, 'tensor')
- refreshed_up_weight: bfloat16 [128, 64, 28672], P('dp', None, 'tensor')
Inputs may be any that keep to these rules, and one draw needn't show every extreme that they name: A permutation. Adapter a is stored at index adapter_storage_index[a] of adapter_down_weight and adapter_up_weight, and the dp index adapter_storage_index[a] // 2 owns it. `decode_adapter_index`: among the rows of one dp index, at most 4 name adapters of one owner. In every draw one owner gets exactly 4 from every dp index. Each dp index also sends exactly 4 to a second owner, which may differ from index to index. `block_adapter_index`: each block names an adapter owned by the dp index that holds the block. The live rows of a block are its first block_live_count rows; the others are padding.
All inputs are finite; a program needn't handle non-finite values.
Results may differ from a plain program's by a relative error of at most 0.0049.
Values may be sent and summed in bfloat16 or wider, within the bound.
A program may use at most 64 MiB of HBM per device.

v0:
```python
import jax
import jax.numpy as jnp
from jax import lax
from jax.sharding import PartitionSpec as P

down_learning_rate = 4.0
up_learning_rate = 0.25


def lookup(table, wanted):
    hits = wanted[:, None] == jnp.arange(table.shape[0], dtype=jnp.int32)[None, :]
    return jnp.sum(jnp.where(hits, table[None, :], 0), axis=1)


def local(
    decode_input_rows,
    decode_adapter_index,
    adapter_storage_index,
    learner_input_rows,
    learner_gradient,
    block_adapter_index,
    block_live_count,
    adapter_down_weight,
    adapter_up_weight,
):
    owners = lax.axis_size("dp")
    split_points = lax.axis_size("tensor")
    holder_mask, rank_extent, width_portion = adapter_down_weight.shape
    hidden_portion = adapter_up_weight.shape[2]
    shrink = (width_portion * split_points) ** (-0.5)
    expand = rank_extent ** (-0.5)
    row_count = decode_input_rows.shape[0]
    slot_depth = 2 * row_count // owners
    total_slots = owners * slot_depth
    slot_row = lookup(adapter_storage_index, decode_adapter_index)
    target = slot_row // holder_mask
    local_slot = slot_row % holder_mask
    target_hot = (target[:, None] == jnp.arange(owners, dtype=jnp.int32)[None, :]).astype(jnp.int32)
    before = jnp.cumsum(target_hot, axis=0) - target_hot
    position = target * slot_depth + jnp.sum(before * target_hot, axis=1)
    matches = jnp.arange(total_slots, dtype=jnp.int32)[:, None] == position[None, :]
    dispatch = matches.astype(jnp.bfloat16)
    send_rows = jnp.dot(dispatch, decode_input_rows, preferred_element_type=jnp.float32).astype(
        jnp.bfloat16
    )
    filled = jnp.any(matches, axis=1)
    send_local = jnp.where(filled, jnp.sum(jnp.where(matches, local_slot[None, :], 0), axis=1), -1)
    send_rows = send_rows.reshape(owners, slot_depth, width_portion)
    send_local = send_local.astype(jnp.bfloat16).reshape(owners, slot_depth)
    flattened_second = adapter_up_weight.reshape(holder_mask * rank_extent, hidden_portion)
    got_rows, got_local = (
        lax.all_to_all(send_rows, "dp", split_axis=0, concat_axis=0, tiled=True),
        lax.all_to_all(send_local, "dp", split_axis=0, concat_axis=0, tiled=True),
    )
    sources, items = got_local.shape
    flattened_rows = got_rows.reshape(sources * items, width_portion)
    which_slot = got_local.reshape(-1).astype(jnp.float32)
    chosen = (which_slot[:, None] == jnp.arange(holder_mask, dtype=jnp.float32)[None, :]).astype(
        jnp.float32
    )
    partial_output = jnp.einsum(
        "lm,kjm->lkj", flattened_rows, adapter_down_weight, preferred_element_type=jnp.float32
    )
    to_sum = partial_output.reshape(sources * items, holder_mask * rank_extent)
    summed = lax.psum(to_sum, "tensor")
    spread = summed.reshape(sources * items, holder_mask, rank_extent) * chosen[:, :, None]
    hidden = (
        (spread * shrink).reshape(sources * items, holder_mask * rank_extent).astype(jnp.bfloat16)
    )
    delta_rows = jnp.dot(hidden, flattened_second, preferred_element_type=jnp.float32) * expand
    answer = delta_rows.astype(jnp.bfloat16).reshape(sources, items, hidden_portion)
    returned = lax.all_to_all(answer, "dp", split_axis=0, concat_axis=0, tiled=True)
    merged = returned.reshape(total_slots, hidden_portion)
    dec_delta = jnp.einsum(
        "mr,mf->rf", dispatch, merged, preferred_element_type=jnp.float32
    ).astype(jnp.bfloat16)
    blocks = block_adapter_index.shape[0]
    length = learner_input_rows.shape[0] // blocks
    block_local = lookup(adapter_storage_index, block_adapter_index) % holder_mask
    block_onehot = block_local[:, None] == jnp.arange(holder_mask, dtype=jnp.int32)[None, :]
    empty_result = jnp.zeros((), jnp.bfloat16)
    gather_down_weight = jnp.sum(
        jnp.where(block_onehot[:, :, None, None], adapter_down_weight[None], empty_result), axis=1
    )
    gather_up_weight = jnp.sum(
        jnp.where(block_onehot[:, :, None, None], adapter_up_weight[None], empty_result), axis=1
    )
    rows_b = learner_input_rows.reshape(blocks, length, width_portion)
    grad_in = learner_gradient.reshape(blocks, length, hidden_portion)
    forward = jnp.einsum(
        "bnd,brd->bnr", rows_b, gather_down_weight, preferred_element_type=jnp.float32
    )
    backward = jnp.einsum(
        "bnf,brf->bnr", grad_in, gather_up_weight, preferred_element_type=jnp.float32
    )
    rank_pair = lax.psum(jnp.concatenate([forward, backward], axis=2), "tensor")
    live_mask = (jnp.arange(length, dtype=jnp.int32)[None, :] < block_live_count[:, None]).astype(
        jnp.float32
    )[:, :, None]
    rank_act = (rank_pair[:, :, :rank_extent] * shrink * live_mask).astype(jnp.bfloat16)
    rank_back = (rank_pair[:, :, rank_extent:] * expand * live_mask).astype(jnp.bfloat16)
    grad_a = (
        jnp.einsum("bnr,bnd->brd", rank_back, rows_b, preferred_element_type=jnp.float32) * shrink
    )
    grad_b = (
        jnp.einsum("bnr,bnf->brf", rank_act, grad_in, preferred_element_type=jnp.float32) * expand
    )
    hot_float = block_onehot.astype(jnp.float32)
    down_gradient_sum = jnp.einsum("bs,brd->srd", hot_float, grad_a)
    up_gradient_sum = jnp.einsum("bs,brf->srf", hot_float, grad_b)
    refreshed_down_weight = (
        adapter_down_weight.astype(jnp.float32) - down_learning_rate * down_gradient_sum
    ).astype(jnp.bfloat16)
    refreshed_up_weight = (
        adapter_up_weight.astype(jnp.float32) - up_learning_rate * up_gradient_sum
    ).astype(jnp.bfloat16)
    return (dec_delta, refreshed_down_weight, refreshed_up_weight)


def solution(mesh):
    in_specs = (
        P("dp", "tensor"),
        P("dp"),
        P(),
        P("dp", "tensor"),
        P("dp", "tensor"),
        P("dp"),
        P("dp"),
        P("dp", None, "tensor"),
        P("dp", None, "tensor"),
    )
    out_specs = (P("dp", "tensor"), P("dp", None, "tensor"), P("dp", None, "tensor"))
    return jax.shard_map(local, mesh=mesh, in_specs=in_specs, out_specs=out_specs, check_vma=False)
```

profile of v0, /device:TPU:24, one launch (start us, length us, event | category | flops | bytes accessed | tf_op | source)
XLA Modules:
  0.0 284.2 jit_solution(16168845379494948341)
XLA Ops:
  7.2 0.9 select_reduce_fusion.4
  8.2 0.2 reduce_window_sum.11
  8.4 0.2 select_reduce_fusion.3
  8.6 0.1 fusion.1
  8.7 0.1 select_reduce_fusion.2
  8.8 0.7 convert_element_type.94
  9.6 18.6 %all-to-all-start.1 = ((bf16[64,1,4]{2,1,0:T(2,128)(2,1)}), bf16[64,1,4]{2,1,0:T(2,128)(2,1)S(1)}, u32[]{:S(2)}, u32[]{:S(2)}) async-start(bf16[64,1,4]{2,1,0:T(2,128)(2,1)} %convert_element_type.94), calls=%async_computation.1 | async-start | bytes 65536 | tf_op jit(solution)/shard_map/all_to_all | solution.py:53
  28.1 1.3 convolution_convert_fusion.1
  29.5 1.1 reshape.215
  30.6 12.1 %all-to-all-done.1 = bf16[64,1,4]{2,1,0:T(2,128)(2,1)S(1)} async-done(((bf16[64,1,4]{2,1,0:T(2,128)(2,1)}), bf16[64,1,4]{2,1,0:T(2,128)(2,1)S(1)}, u32[]{:S(2)}, u32[]{:S(2)}) %all-to-all-start.1) | async-done | bytes 544 | tf_op jit(solution)/shard_map/all_to_all | solution.py:53
  42.7 4.6 %all-to-all-start = ((bf16[64,4,1536]{2,1,0:T(4,128)(2,1)}), bf16[64,4,1536]{2,1,0:T(4,128)(2,1)S(1)}, u32[]{:S(2)}, u32[]{:S(2)}) async-start(bf16[64,4,1536]{2,1,0:T(4,128)(2,1)} %reshape.215), calls=%async_computation | async-start | bytes 1572864 | tf_op jit(solution)/shard_map/all_to_all | solution.py:52
  48.0 0.6 fusion.14
  50.6 0.1 select_reduce_fusion.1
  50.8 0.2 convolution_bitcast_fusion.1
  51.1 0.3 select_reduce_fusion
  51.4 0.4 convolution_bitcast_fusion
  51.8 0.6 pad_maximum_fusion
  52.6 0.1 reshape.222
  52.7 37.5 %all-to-all-done = bf16[64,4,1536]{2,1,0:T(4,128)(2,1)S(1)} async-done(((bf16[64,4,1536]{2,1,0:T(4,128)(2,1)}), bf16[64,4,1536]{2,1,0:T(4,128)(2,1)S(1)}, u32[]{:S(2)}, u32[]{:S(2)}) %all-to-all-start) | async-done | bytes 786464 | tf_op jit(solution)/shard_map/all_to_all | solution.py:52
  90.2 1.1 reshape.216
  91.3 2.1 fusion.17
  93.6 64.4 %all-reduce.3.cloned.1.call-done = (f32[256,128]{1,0:T(8,128)}, f32[1,128,128]{1,2,0:T(8,128)}) async-done(((f32[256,128]{1,0:T(8,128)}, f32[1,128,128]{1,2,0:T(8,128)}), (f32[256,128]{1,0:T(8,128)}, f32[1,128,128]{1,2,0:T(8,128)})) %all-reduce.3.cloned.1.call-update) | async-done | bytes 196624 | tf_op jit(solution)/shard_map/psum | solution.py:65
  158.0 2.8 fusion
  160.8 4.1 %reshape.218 = bf16[64,4,3584]{2,1,0:T(4,128)(2,1)} reshape(bf16[256,3584]{1,0:T(8,128)(2,1)} %fusion) | data formatting | bytes 3670016 | tf_op jit(solution)/shard_map/reshape | solution.py:71
  164.9 16.0 %all-to-all-start.2 = ((bf16[64,4,3584]{2,1,0:T(4,128)(2,1)}), bf16[64,4,3584]{2,1,0:T(4,128)(2,1)}, u32[]{:S(2)}, u32[]{:S(2)}) async-start(bf16[64,4,3584]{2,1,0:T(4,128)(2,1)} %reshape.218), calls=%async_computation.2 | async-start | bytes 3670016 | tf_op jit(solution)/shard_map/all_to_all | solution.py:72
  181.5 0.2 convolution_multiply_fusion.2
  181.7 0.3 convolution_multiply_fusion.1
  182.0 0.9 subtract_convert_fusion.1
  182.9 1.3 subtract_convert_fusion
  184.2 86.4 %all-to-all-done.2 = bf16[64,4,3584]{2,1,0:T(4,128)(2,1)} async-done(((bf16[64,4,3584]{2,1,0:T(4,128)(2,1)}), bf16[64,4,3584]{2,1,0:T(4,128)(2,1)}, u32[]{:S(2)}, u32[]{:S(2)}) %all-to-all-start.2) | async-done | bytes 1835040 | tf_op jit(solution)/shard_map/all_to_all | solution.py:72
  270.6 3.9 %reshape.219 = bf16[256,3584]{1,0:T(8,128)(2,1)} reshape(bf16[64,4,3584]{2,1,0:T(4,128)(2,1)} %all-to-all-done.2) | data formatting | bytes 3670016 | tf_op jit(solution)/shard_map/reshape | solution.py:73
  274.5 2.9 %convolution_convert_fusion = bf16[128,3584]{1,0:T(8,128)(2,1)} fusion(bf16[256,3584]{1,0:T(8,128)(2,1)} %reshape.219, s32[128]{0:T(128)S(1)} %multiply_add_fusion), kind=kOutput, calls=%fused_computation.2 | convolution fusion | flops 235372544 | bytes 2753024 | tf_op jit(solution)/shard_map/mr,mf->rf/dot_general | solution.py:74
  (25 shorter events, 0.4 us)
Async XLA Ops:
  7.2 44.2 %copy-start = (bf16[128,3584]{1,0:T(8,128)(2,1)S(1)}, bf16[128,3584]{1,0:T(8,128)(2,1)}, u32[]{:S(2)}) copy-start(bf16[128,3584]{1,0:T(8,128)(2,1)} %param.13) | copy-start | bytes 2752516
  9.6 33.1 %all-to-all-start.1 = ((bf16[64,1,4]{2,1,0:T(2,128)(2,1)}), bf16[64,1,4]{2,1,0:T(2,128)(2,1)S(1)}, u32[]{:S(2)}, u32[]{:S(2)}) async-start(bf16[64,1,4]{2,1,0:T(2,128)(2,1)} %convert_element_type.94), calls=%async_computation.1 | async-start | bytes 65536 | tf_op jit(solution)/shard_map/all_to_all | solution.py:53
  29.5 18.5 %copy-start.5 = (s32[128]{0:T(128)S(1)}, s32[128]{0:T(128)}, u32[]{:S(2)}) copy-start(s32[128]{0:T(128)} %param.11) | copy-start | bytes 1540
  29.5 21.1 %copy-start.2 = (bf16[2,64,1536]{2,1,0:T(8,128)(2,1)S(1)}, bf16[2,64,1536]{2,1,0:T(8,128)(2,1)}, u32[]{:S(2)}) copy-start(bf16[2,64,1536]{2,1,0:T(8,128)(2,1)} %param.16) | copy-start | bytes 1179652
  29.5 21.3 %copy-start.3 = (bf16[128,1536]{1,0:T(8,128)(2,1)S(1)}, bf16[128,1536]{1,0:T(8,128)(2,1)}, u32[]{:S(2)}) copy-start(bf16[128,1536]{1,0:T(8,128)(2,1)} %param.12) | copy-start | bytes 1179652
  29.5 21.5 %copy-start.1 = (bf16[2,64,3584]{2,1,0:T(8,128)(2,1)S(1)}, bf16[2,64,3584]{2,1,0:T(8,128)(2,1)}, u32[]{:S(2)}) copy-start(bf16[2,64,3584]{2,1,0:T(8,128)(2,1)} %param.17) | copy-start | bytes 2752516
  42.7 47.6 %all-to-all-start = ((bf16[64,4,1536]{2,1,0:T(4,128)(2,1)}), bf16[64,4,1536]{2,1,0:T(4,128)(2,1)S(1)}, u32[]{:S(2)}, u32[]{:S(2)}) async-start(bf16[64,4,1536]{2,1,0:T(4,128)(2,1)} %reshape.215), calls=%async_computation | async-start | bytes 1572864 | tf_op jit(solution)/shard_map/all_to_all | solution.py:52
  47.3 110.7 %all-reduce.3.cloned.1.call-start = ((), (), s32[]{:S(2)}) async-start(), calls=%async_computation.3 | async-start | bytes 393216 | tf_op jit(solution)/shard_map/psum | solution.py:65
  164.9 16.7 %copy-start.4 = (f32[1,128,128]{1,2,0:T(8,128)S(1)}, f32[1,128,128]{1,2,0:T(8,128)}, u32[]{:S(2)}) copy-start(f32[1,128,128]{1,2,0:T(8,128)} %get-tuple-element.4) | copy-start | bytes 196612
  164.9 105.7 %all-to-all-start.2 = ((bf16[64,4,3584]{2,1,0:T(4,128)(2,1)}), bf16[64,4,3584]{2,1,0:T(4,128)(2,1)}, u32[]{:S(2)}, u32[]{:S(2)}) async-start(bf16[64,4,3584]{2,1,0:T(4,128)(2,1)} %reshape.218), calls=%async_computation.2 | async-start | bytes 3670016 | tf_op jit(solution)/shard_map/all_to_all | solution.py:72
Sparse Core Ops, SparseCore 0:
  93.6 64.3 all-reduce.2
where the time goes:
time: 285 us; the launch traced here: 284 us
  waiting for transfers between devices  200 us (70%)
  starting transfers between devices  39.2 us (14%)
  between operations  17.5 us (6%)
  local copies, waits for them, and re-layouts  11.1 us (4%)
  matrix products  10.3 us (4%)
  other arithmetic  5.69 us (2%)
    all_to_all x1, waiting for transfers between devices, local(): lax.all_to_all(answer, 'dp', split_axis=0, concat_axis=0, tiled=True)  86.4 us
    psum x1, waiting for transfers between devices, local(): summed = lax.psum(to_sum, 'tensor')  64.4 us
    all_to_all x1, waiting for transfers between devices, local(): lax.all_to_all(send_rows, 'dp', split_axis=0, concat_axis=0, tiled=True)  37.5 us
    all_to_all x1, starting transfers between devices, local(): lax.all_to_all(send_local, 'dp', split_axis=0, concat_axis=0, tiled=True)  18.6 us
    all_to_all x1, starting transfers between devices, local(): lax.all_to_all(answer, 'dp', split_axis=0, concat_axis=0, tiled=True)  16 us
    all_to_all x1, waiting for transfers between devices, local(): lax.all_to_all(send_local, 'dp', split_axis=0, concat_axis=0, tiled=True)  12.1 us
  transfers between devices with their start and end apart: 4, of which 4 were waited for; matrix products, arithmetic and copies ran while one was open for 3% of the time, Pallas kernels for 0%

commit v1 on v0

v1 whole, which is shorter than its diff:
```python
import functools

import jax
import jax.numpy as jnp
from jax import lax
from jax.experimental import pallas as pl
from jax.experimental.pallas import tpu as pltpu
from jax.sharding import PartitionSpec as P

DOWN_RATE = 4.0
UP_RATE = 0.25
DEPTH = 4
CHUNKS = 4
BLOCK = DEPTH * CHUNKS
MESH = pl.DeviceIdType.MESH
F32, BF16, I32 = jnp.float32, jnp.bfloat16, jnp.int32


def nt_dot(a, b):
    return lax.dot_general(a, b, (((1,), (1,)), ((), ())), preferred_element_type=F32)


def tn_dot(a, b):
    return lax.dot_general(a, b, (((0,), (0,)), ((), ())), preferred_element_type=F32)


def nn_dot(a, b):
    return jnp.dot(a, b, preferred_element_type=F32)


def iota(shape, axis):
    return lax.broadcasted_iota(I32, shape, axis)


def kernel(
    geometry,
    dec_index_ref,
    store_ref,
    store_s_ref,
    blk_s_ref,
    live_s_ref,
    dec_hbm,
    rows_hbm,
    grad_hbm,
    down_hbm,
    up_hbm,
    delta_out,
    down_out,
    up_out,
    dec,
    rows,
    grad,
    down,
    up,
    send,
    got,
    meta2,
    meta_send,
    meta_got,
    part,
    part_got,
    lpart,
    lpart_got,
    dsend,
    dgot,
    total,
    load_sems,
    send_sem,
    got_sems,
    meta_send_sem,
    meta_got_sems,
    part_send_sem,
    part_got_sems,
    lpart_send_sem,
    lpart_got_sem,
    dsend_sem,
    dgot_sems,
):
    zs, xs, ts, shrink, expand = geometry
    owners = zs * xs
    wide = 2 * xs
    groups = zs // 2
    gr = wide * BLOCK
    me = lax.axis_index("dp")
    t = lax.axis_index("tensor")
    z, x = me // xs, me % xs
    count = dec.shape[0]
    wc = dec.shape[1] // CHUNKS
    hc = grad.shape[1] // CHUNKS

    def offset(i):
        k = i // wide
        half = (i % wide) // xs
        dz = k + half * (zs - 2 * k - (zs // 2) * ((zs - k) // zs))
        return dz, i % xs

    def owner_of(i):
        dz, dx = offset(i)
        return ((z + dz) % zs) * xs + (x + dx) % xs

    def source_of(i):
        dz, dx = offset(i)
        return ((z + zs - dz) % zs) * xs + (x + xs - dx) % xs

    def load(k, src, dst):
        return pltpu.make_async_copy(src, dst, load_sems.at[k])

    loads = [
        load(0, dec_hbm, dec),
        load(1, rows_hbm, rows),
        load(2, down_hbm, down),
        load(3, grad_hbm, grad),
        load(4, up_hbm, up),
    ]
    for one in loads:
        one.start()

    barrier = pltpu.get_barrier_semaphore()

    def greet(i, carry):
        pl.semaphore_signal(barrier, inc=1, device_id=(owner_of(i), t), device_id_type=MESH)
        return carry

    lax.fori_loop(1, owners, greet, 0)

    def greet_t(j, carry):
        pl.semaphore_signal(barrier, inc=1, device_id=(me, (t + j) % ts), device_id_type=MESH)
        return carry

    lax.fori_loop(1, ts, greet_t, 0)

    adapters = store_ref.shape[1]
    hits = (iota((adapters, count), 0) == dec_index_ref[...]).astype(F32).astype(BF16)
    table = jnp.broadcast_to(store_ref[...], (8, adapters)).astype(F32).astype(BF16)
    slot = nn_dot(table, hits)[0:1].astype(I32)
    owner, local = slot // 2, slot % 2
    dz = (owner // xs - z + zs) % zs
    dx = (owner % xs - x + xs) % xs
    half = (dz >= zs // 2).astype(I32)
    k = jnp.where(dz < zs // 2, dz, jnp.where(dz == zs // 2, 0, zs - dz))
    block = k * wide + half * xs + dx
    square = (count, count)
    block_rows = jnp.broadcast_to(block, square)
    block_cols = jnp.transpose(block_rows.astype(F32)).astype(I32)
    same = jnp.logical_and(block_rows == block_cols, iota(square, 0) < iota(square, 1))
    before = jnp.sum(same.astype(F32), axis=0, keepdims=True).astype(I32)
    place = block * BLOCK + before
    code = jnp.broadcast_to(place * 2 + local, square)
    code_cols = jnp.transpose(code.astype(F32)).astype(I32)
    place_cols = code_cols // 2
    named = (code_cols % 2 + 1).astype(F32)
    lanes = iota((count, 128), 1)
    slot_cols = jnp.broadcast_to(place_cols[:, 0:1] % BLOCK, (count, 128))
    spread = jnp.where(
        lanes % DEPTH == slot_cols, jnp.broadcast_to(named[:, 0:1], (count, 128)), 0.0
    )
    in_block = (iota((owners, count), 0) == block).astype(F32).astype(BF16)
    meta2[...] = nn_dot(in_block, spread.astype(BF16))

    def lift(i, carry):
        meta_send[i] = meta2[pl.ds(i, 1), :]
        return carry

    lax.fori_loop(0, owners, lift, 0)
    meta_got[0] = meta2[0:1, :]

    loads[0].wait()
    pl.semaphore_wait(barrier, owners - 1 + ts - 1)

    def row_copy(i):
        at = pl.ds(pl.multiple_of(i * BLOCK, BLOCK), BLOCK)
        return pltpu.make_async_remote_copy(
            src_ref=send.at[at],
            dst_ref=got.at[at],
            send_sem=send_sem,
            recv_sem=got_sems.at[i // wide],
            device_id=(owner_of(i), t),
            device_id_type=MESH,
        )

    def meta_copy(i):
        return pltpu.make_async_remote_copy(
            src_ref=meta_send.at[i],
            dst_ref=meta_got.at[i],
            send_sem=meta_send_sem,
            recv_sem=meta_got_sems.at[i // wide],
            device_id=(owner_of(i), t),
            device_id_type=MESH,
        )

    def start_rows(i, carry):
        meta_copy(i).start()
        row_copy(i).start()
        return carry

    def dispatch(g):
        base = pl.multiple_of(g * gr, gr)
        rel = iota((gr, count), 0) + base
        sum_rows = jnp.zeros((gr, wc), F32)
        for c in range(CHUNKS):
            chosen = (rel == place + c * DEPTH).astype(F32).astype(BF16)
            sum_rows += nn_dot(chosen, dec[:, c * wc : (c + 1) * wc])
        send[pl.ds(base, gr), :] = sum_rows.astype(BF16)

    dispatch(0)
    lax.fori_loop(1, wide, start_rows, 0)
    got[0:BLOCK, :] = send[0:BLOCK, :]

    def dispatch_more(g, carry):
        dispatch(g)
        lax.fori_loop(g * wide, (g + 1) * wide, start_rows, 0)
        return carry

    lax.fori_loop(1, groups, dispatch_more, 0)

    rank = down.shape[0] // 2
    learn = rows.shape[0]
    own_slot = store_s_ref[blk_s_ref[0]] % 2
    aj = iota((learn, 2 * rank), 1)
    own = (aj // rank == own_slot).astype(F32)
    loads[1].wait()
    loads[2].wait()
    forward = nt_dot(rows[...], down[...]) * own
    loads[3].wait()
    loads[4].wait()
    backward = nt_dot(grad[...], up[...]) * own
    forward = forward + pltpu.roll(forward, rank, 1)
    backward = backward + pltpu.roll(backward, rank, 1)
    lpart[...] = jnp.where(aj < rank, forward, backward)

    def lpart_copy(j):
        return pltpu.make_async_remote_copy(
            src_ref=lpart,
            dst_ref=lpart_got.at[j - 1],
            send_sem=lpart_send_sem,
            recv_sem=lpart_got_sem,
            device_id=(me, (t + j) % ts),
            device_id_type=MESH,
        )

    def start_lpart(j, carry):
        lpart_copy(j).start()
        return carry

    lax.fori_loop(1, ts, start_lpart, 0)

    def wait_group(g, ref, size, sems):
        @pl.when(g == 0)
        def _():
            view = ref.at[pl.ds(size, (wide - 1) * size)]
            pltpu.make_async_copy(view, view, sems.at[g]).wait()

        @pl.when(g > 0)
        def _():
            view = ref.at[pl.ds(pl.multiple_of(g * wide * size, wide * size), wide * size)]
            pltpu.make_async_copy(view, view, sems.at[g]).wait()

    chunk_of = (iota((gr, 2 * rank), 0) % BLOCK) // DEPTH
    lane = iota((gr, 2 * rank), 1)

    def chosen_mask(g):
        ids = meta_got[pl.ds(g * wide, wide)]
        ids = jnp.broadcast_to(ids, (wide, BLOCK, 128)).reshape(gr, 128)
        mine = iota((gr, 128), 1) == iota((gr, 128), 0) % DEPTH
        which = jnp.sum(jnp.where(mine, ids, 0.0), axis=1, keepdims=True)
        return (which == (lane // rank + 1).astype(F32)).astype(F32)

    pairs = wide // 2
    top3 = iota((wide, 8, 2 * rank), 1) < DEPTH
    left3 = iota((wide, 8, 2 * rank), 2) < rank

    def part_copy(g, j):
        return pltpu.make_async_remote_copy(
            src_ref=part.at[g],
            dst_ref=part_got.at[g, j - 1],
            send_sem=part_send_sem,
            recv_sem=part_got_sems.at[g],
            device_id=(me, (t + j) % ts),
            device_id_type=MESH,
        )

    def ranks(g):
        wait_group(g, got, BLOCK, got_sems)
        wait_group(g, meta_got, 1, meta_got_sems)
        at = pl.ds(pl.multiple_of(g * gr, gr), gr)
        block_rows = got[at, :]
        both = jnp.zeros((gr, 2 * rank), F32)
        for c in range(CHUNKS):
            one = nt_dot(block_rows, down[:, c * wc : (c + 1) * wc])
            both = both + jnp.where(chunk_of == c, one, 0.0)
        both = both * chosen_mask(g)
        both = both.reshape(wide, 2, 8, 2 * rank)
        both = both[:, 0] + both[:, 1]
        both = both + pltpu.roll(both, DEPTH, 1)
        both = both + pltpu.roll(both, rank, 2)
        both = both.reshape(2, pairs, 8, 2 * rank)
        two = jnp.where(top3[:pairs], both[0], both[1])
        two = two.reshape(2, pairs // 2, 8, 2 * rank)
        part[g] = jnp.where(left3[: pairs // 2], two[0], two[1])

        def start(j, carry):
            part_copy(g, j).start()
            return carry

        lax.fori_loop(1, ts, start, 0)

    def delta_copy(i):
        at = pl.ds(pl.multiple_of(i * BLOCK, BLOCK), BLOCK)
        return pltpu.make_async_remote_copy(
            src_ref=dsend.at[at],
            dst_ref=dgot.at[at],
            send_sem=dsend_sem,
            recv_sem=dgot_sems.at[i // wide],
            device_id=(source_of(i), t),
            device_id_type=MESH,
        )

    def start_delta(i, carry):
        delta_copy(i).start()
        return carry

    def deltas(g):
        view = part_got.at[g]
        pltpu.make_async_copy(view, view, part_got_sems.at[g]).wait()
        v = part[g]
        for j in range(ts - 1):
            v = v + part_got[g, j]
        v = (v * shrink).astype(BF16).astype(F32)
        turned = pltpu.roll(v, rank, 2)
        keep = left3[: pairs // 2]
        two = jnp.concatenate([jnp.where(keep, v, turned), jnp.where(keep, turned, v)], axis=0)
        turned = pltpu.roll(two, DEPTH, 1)
        keep = top3[:pairs]
        both = jnp.concatenate([jnp.where(keep, two, turned), jnp.where(keep, turned, two)], axis=0)
        both = jnp.broadcast_to(both[:, None], (wide, 2, 8, 2 * rank)).reshape(gr, 2 * rank)
        both = both * chosen_mask(g)
        base = pl.multiple_of(g * gr, gr)
        sum_rows = jnp.zeros((gr, hc), F32)
        for c in range(CHUNKS):
            left = jnp.where(chunk_of == c, both, 0.0).astype(BF16)
            sum_rows += nn_dot(left, up[:, c * hc : (c + 1) * hc])
        dsend[pl.ds(base, gr), :] = (sum_rows * expand).astype(BF16)

        @pl.when(g == 0)
        def _():
            dgot[0:BLOCK, :] = dsend[0:BLOCK, :]
            lax.fori_loop(1, wide, start_delta, 0)

        @pl.when(g > 0)
        def _():
            lax.fori_loop(g * wide, (g + 1) * wide, start_delta, 0)

    ranks(0)

    def step(g, carry):
        ranks(g)
        deltas(g - 1)
        return carry

    lax.fori_loop(1, groups, step, 0)
    deltas(groups - 1)

    pltpu.make_async_copy(lpart_got, lpart_got, lpart_got_sem).wait()
    v = lpart[...]
    for j in range(ts - 1):
        v = v + lpart_got[j]
    live = (iota((learn, 2 * rank), 0) < live_s_ref[0]).astype(F32)
    scale = jnp.where(aj < rank, shrink, expand)
    v = (v * scale * live).astype(BF16).astype(F32)
    turned = pltpu.roll(v, rank, 1)
    act = (jnp.where(aj < rank, v, turned) * own).astype(BF16)
    back = (jnp.where(aj < rank, turned, v) * own).astype(BF16)
    for c in range(CHUNKS):
        at = slice(c * wc, (c + 1) * wc)
        g_a = tn_dot(back, rows[:, at]) * shrink
        down_out[:, at] = (down[:, at].astype(F32) - DOWN_RATE * g_a).astype(BF16)
    for c in range(CHUNKS):
        at = slice(c * hc, (c + 1) * hc)
        g_b = tn_dot(act, grad[:, at]) * expand
        up_out[:, at] = (up[:, at].astype(F32) - UP_RATE * g_b).astype(BF16)

    total[...] = jnp.zeros_like(total)
    place_128 = jnp.broadcast_to(place_cols[:, 0:1], (count, gr))

    def combine(g, carry):
        wait_group(g, dgot, BLOCK, dgot_sems)
        base = pl.multiple_of(g * gr, gr)
        rel = iota((count, gr), 1) + base
        arrived = dgot[pl.ds(base, gr), :]
        for c in range(CHUNKS):
            chosen = (rel == place_128 + c * DEPTH).astype(F32).astype(BF16)
            total[:, c * hc : (c + 1) * hc] += nn_dot(chosen, arrived)
        return carry

    lax.fori_loop(0, groups, combine, 0)
    delta_out[...] = total[...].astype(BF16)

    def drain(view, sem):
        pltpu.make_async_copy(view, view, sem).wait()

    drain(send.at[pl.ds(BLOCK, (owners - 1) * BLOCK)], send_sem)
    drain(meta_send.at[pl.ds(1, owners - 1)], meta_send_sem)
    drain(dsend.at[pl.ds(BLOCK, (owners - 1) * BLOCK)], dsend_sem)
    drain(lpart_got, lpart_send_sem)
    drain(part_got, part_send_sem)


def local(
    decode_input_rows,
    decode_adapter_index,
    adapter_storage_index,
    learner_input_rows,
    learner_gradient,
    block_adapter_index,
    block_live_count,
    adapter_down_weight,
    adapter_up_weight,
):
    owners = lax.axis_size("dp")
    ts = lax.axis_size("tensor")
    xs = 4
    zs = owners // xs
    held, rank, width = adapter_down_weight.shape
    hidden = adapter_up_weight.shape[2]
    count = decode_input_rows.shape[0]
    learn = learner_input_rows.shape[0]
    shrink = (width * ts) ** (-0.5)
    expand = rank ** (-0.5)
    groups = zs // 2
    wide = 2 * xs
    vmem = pl.BlockSpec(memory_space=pltpu.VMEM)
    smem = pl.BlockSpec(memory_space=pltpu.SMEM)
    hbm = pl.BlockSpec(memory_space=pl.ANY)
    dma = pltpu.SemaphoreType.DMA
    packed = (wide // 4, 8, 2 * rank)
    delta, down, up = pl.pallas_call(
        functools.partial(kernel, (zs, xs, ts, shrink, expand)),
        out_shape=(
            jax.ShapeDtypeStruct((count, hidden), BF16),
            jax.ShapeDtypeStruct((held * rank, width), BF16),
            jax.ShapeDtypeStruct((held * rank, hidden), BF16),
        ),
        in_specs=[vmem, vmem, smem, smem, smem, hbm, hbm, hbm, hbm, hbm],
        out_specs=(vmem, vmem, vmem),
        scratch_shapes=[
            pltpu.VMEM((count, width), BF16),
            pltpu.VMEM((learn, width), BF16),
            pltpu.VMEM((learn, hidden), BF16),
            pltpu.VMEM((held * rank, width), BF16),
            pltpu.VMEM((held * rank, hidden), BF16),
            pltpu.VMEM((owners * BLOCK, width // CHUNKS), BF16),
            pltpu.VMEM((owners * BLOCK, width // CHUNKS), BF16),
            pltpu.VMEM((owners, 128), F32),
            pltpu.VMEM((owners, 1, 128), F32),
            pltpu.VMEM((owners, 1, 128), F32),
            pltpu.VMEM((groups,) + packed, F32),
            pltpu.VMEM((groups, ts - 1) + packed, F32),
            pltpu.VMEM((learn, 2 * rank), F32),
            pltpu.VMEM((ts - 1, learn, 2 * rank), F32),
            pltpu.VMEM((owners * BLOCK, hidden // CHUNKS), BF16),
            pltpu.VMEM((owners * BLOCK, hidden // CHUNKS), BF16),
            pltpu.VMEM((count, hidden), F32),
            dma((5,)),
            dma,
            dma((groups,)),
            dma,
            dma((groups,)),
            dma,
            dma((groups,)),
            dma,
            dma,
            dma,
            dma((groups,)),
        ],
        compiler_params=pltpu.CompilerParams(
            collective_id=0, has_side_effects=True, vmem_limit_bytes=48 * 1024 * 1024
        ),
    )(
        decode_adapter_index.reshape(1, count),
        adapter_storage_index.reshape(1, -1),
        adapter_storage_index,
        block_adapter_index,
        block_live_count,
        decode_input_rows,
        learner_input_rows,
        learner_gradient,
        adapter_down_weight.reshape(held * rank, width),
        adapter_up_weight.reshape(held * rank, hidden),
    )
    return delta, down.reshape(held, rank, width), up.reshape(held, rank, hidden)


def solution(mesh):
    in_specs = (
        P("dp", "tensor"),
        P("dp"),
        P(),
        P("dp", "tensor"),
        P("dp", "tensor"),
        P("dp"),
        P("dp"),
        P("dp", None, "tensor"),
        P("dp", None, "tensor"),
    )
    out_specs = (P("dp", "tensor"), P("dp", None, "tensor"), P("dp", None, "tensor"))
    return jax.shard_map(local, mesh=mesh, in_specs=in_specs, out_specs=out_specs, check_vma=False)
```

time: 285 us -> 150 us (0.53)
  waiting for transfers between devices: 200 us -> 0 us
  Pallas kernels: 0 us -> 137 us
  starting transfers between devices: 39.2 us -> 0 us
  between operations: 17.5 us -> 1.96 us
  matrix products: 10.3 us -> 0 us
  other arithmetic: 5.69 us -> 0 us
    pallas_call x0 -> x1, Pallas kernels: none -> 137 us  [local(): pl.pallas_call(functools.partial(kernel, (zs, xs, ts, shrink, expand)), o...]
    all_to_all x3 -> x0, waiting for transfers between devices: 136 us -> none  [the longest x1 86.4 us: local(): lax.all_to_all(answer, 'dp', split_axis=0, concat_axis=0, tiled=True)]
    psum x1 -> x0, waiting for transfers between devices: 64.4 us -> none  [local(): summed = lax.psum(to_sum, 'tensor')]
    all_to_all x3 -> x0, starting transfers between devices: 39.2 us -> none  [the longest x1 18.6 us: local(): lax.all_to_all(send_local, 'dp', split_axis=0, concat_axis=0, tiled=True)]
    dot_general x8 -> x0, matrix products: 10.3 us -> none  [the longest x1 2.88 us: local(): jnp.einsum('mr,mf->rf', dispatch, merged, preferred_element_type=jnp.floa...]
    reshape x4 -> x0, local copies, waits for them, and re-layouts: 10.1 us -> none  [the longest x1 4.06 us: local(): delta_rows.astype(jnp.bfloat16).reshape(sources, items, hidden_portion)]
    unnamed x12 -> x17, local copies, waits for them, and re-layouts: 0.04 us -> 8.59 us
  transfers between devices with their start and end apart: 4 -> 0, of which waited for: 4 -> 0; matrix products, arithmetic and copies ran while one was open for 3% -> 0% of each run, Pallas kernels for 0% -> 0%
where the time goes in v1:
time: 150 us; the launch traced here: 147 us
  Pallas kernels  137 us (91%)
  local copies, waits for them, and re-layouts  8.59 us (6%)
  between operations  1.96 us (1%)
    pallas_call x1, Pallas kernels, local(): pl.pallas_call(functools.partial(kernel, (zs, xs, ts, shrink, expand)), o...  137 us
    unnamed x17, local copies, waits for them, and re-layouts  8.59 us

profile of v1, /device:TPU:24, one launch (start us, length us, event | category | flops | bytes accessed | tf_op | source)
XLA Modules:
  0.0 147.4 jit_solution(2409382627075579693)
XLA Ops:
  1.9 0.0 copy-start.5
  1.9 0.0 copy-start.6
  1.9 0.6 copy-done.5
  2.6 0.0 copy-done.6
  2.6 0.0 copy-start
  2.6 1.2 copy-done
  3.8 0.0 copy-start.1
  3.8 1.2 copy-done.1
  5.0 0.0 copy-start.2
  5.0 1.0 copy-done.2
  6.0 0.0 copy-start.3
  6.0 1.0 copy-done.3
  6.9 0.0 copy-start.4
  7.0 1.0 copy-done.4
  7.9 136.9 %shard_map.112 = (bf16[128,3584]{1,0:T(8,128)(2,1)S(1)}, bf16[128,1536]{1,0:T(8,128)(2,1)S(1)}, bf16[128,3584]{1,0:T(8,128)(2,1)S(1)}) custom-call(s32[1,128]{1,0:T(1,128)S(1)} %bitcast.11, s32[1,128]{1,0:T(1,128)S(1)} %bitcast.10, s32[128]{0:T(128)S(1)} %copy-done.5, s32[1]{0:T(128)S(6)} %copy.15.blk_s_ref, s32[1]{0:T(128)S(6)} %copy.16.live_s_ref, ...), custom_call_target="tpu_custom_call" | custom-call | tf_op jit(solution)/shard_map/pallas_call | solution.py:436
  144.8 0.9 copy.17
  145.8 0.7 copy.18
  146.5 0.9 copy.19
Async XLA Ops:
  1.9 0.7 copy-start.5
  1.9 0.7 copy-start.6
  2.6 1.2 copy-start
  3.8 1.2 copy-start.1
  5.0 1.0 copy-start.2
  6.0 1.0 copy-start.3
  6.9 1.0 copy-start.4

commit v2 on v1

--- a/solution.py
+++ b/solution.py
@@ -34,11 +34,11 @@
 
 def kernel(
     geometry,
-    dec_index_ref,
-    store_ref,
-    store_s_ref,
-    blk_s_ref,
-    live_s_ref,
+    dec_index_hbm,
+    store_hbm,
+    store_flat_hbm,
+    blk_hbm,
+    live_hbm,
     dec_hbm,
     rows_hbm,
     grad_hbm,
@@ -47,6 +47,11 @@
     delta_out,
     down_out,
     up_out,
+    dec_index_ref,
+    store_ref,
+    store_s_ref,
+    blk_s_ref,
+    live_s_ref,
     dec,
     rows,
     grad,
@@ -111,7 +116,13 @@
         load(2, down_hbm, down),
         load(3, grad_hbm, grad),
         load(4, up_hbm, up),
+        load(5, dec_index_hbm, dec_index_ref),
+        load(6, store_hbm, store_ref),
+        load(7, store_flat_hbm, store_s_ref),
+        load(8, blk_hbm, blk_s_ref),
+        load(9, live_hbm, live_s_ref),
     ]
+    loads = loads[:1] + loads[5:] + loads[1:5]
     for one in loads:
         one.start()
 
@@ -128,6 +139,9 @@
         return carry
 
     lax.fori_loop(1, ts, greet_t, 0)
+
+    for one in loads[1:6]:
+        one.wait()
 
     adapters = store_ref.shape[1]
     hits = (iota((adapters, count), 0) == dec_index_ref[...]).astype(F32).astype(BF16)
@@ -218,11 +232,11 @@
     own_slot = store_s_ref[blk_s_ref[0]] % 2
     aj = iota((learn, 2 * rank), 1)
     own = (aj // rank == own_slot).astype(F32)
-    loads[1].wait()
-    loads[2].wait()
+    loads[6].wait()
+    loads[7].wait()
     forward = nt_dot(rows[...], down[...]) * own
-    loads[3].wait()
-    loads[4].wait()
+    loads[8].wait()
+    loads[9].wait()
     backward = nt_dot(grad[...], up[...]) * own
     forward = forward + pltpu.roll(forward, rank, 1)
     backward = backward + pltpu.roll(backward, rank, 1)
@@ -429,8 +443,7 @@
     groups = zs // 2
     wide = 2 * xs
     vmem = pl.BlockSpec(memory_space=pltpu.VMEM)
-    smem = pl.BlockSpec(memory_space=pltpu.SMEM)
-    hbm = pl.BlockSpec(memory_space=pl.ANY)
+    hbm = pl.BlockSpec(memory_space=pltpu.HBM)
     dma = pltpu.SemaphoreType.DMA
     packed = (wide // 4, 8, 2 * rank)
     delta, down, up = pl.pallas_call(
@@ -440,9 +453,14 @@
             jax.ShapeDtypeStruct((held * rank, width), BF16),
             jax.ShapeDtypeStruct((held * rank, hidden), BF16),
         ),
-        in_specs=[vmem, vmem, smem, smem, smem, hbm, hbm, hbm, hbm, hbm],
+        in_specs=[hbm] * 10,
         out_specs=(vmem, vmem, vmem),
         scratch_shapes=[
+            pltpu.VMEM((1, count), I32),
+            pltpu.VMEM((1, adapter_storage_index.shape[0]), I32),
+            pltpu.SMEM((adapter_storage_index.shape[0],), I32),
+            pltpu.SMEM((1,), I32),
+            pltpu.SMEM((1,), I32),
             pltpu.VMEM((count, width), BF16),
             pltpu.VMEM((learn, width), BF16),
             pltpu.VMEM((learn, hidden), BF16),
@@ -460,7 +478,7 @@
             pltpu.VMEM((owners * BLOCK, hidden // CHUNKS), BF16),
             pltpu.VMEM((owners * BLOCK, hidden // CHUNKS), BF16),
             pltpu.VMEM((count, hidden), F32),
-            dma((5,)),
+            dma((10,)),
             dma,
             dma((groups,)),
             dma,
@@ -473,7 +491,7 @@
             dma((groups,)),
         ],
         compiler_params=pltpu.CompilerParams(
-            collective_id=0, has_side_effects=True, vmem_limit_bytes=48 * 1024 * 1024
+            collective_id=0, has_side_effects=True, vmem_limit_bytes=58 * 1024 * 1024
         ),
     )(
         decode_adapter_index.reshape(1, count),

time: 150 us -> 145 us (0.967)
  local copies, waits for them, and re-layouts: 8.59 us -> 3.94 us
    unnamed x17 -> x7, local copies, waits for them, and re-layouts: 8.59 us -> 3.94 us
where the time goes in v2:
time: 145 us; the launch traced here: 143 us
  Pallas kernels  137 us (94%)
  local copies, waits for them, and re-layouts  3.94 us (3%)
  between operations  1.95 us (1%)
    pallas_call x1, Pallas kernels, local(): pl.pallas_call(functools.partial(kernel, (zs, xs, ts, shrink, expand)), o...  137 us
    unnamed x7, local copies, waits for them, and re-layouts  3.94 us

profile of v2, /device:TPU:24, one launch (start us, length us, event | category | flops | bytes accessed | tf_op | source)
XLA Modules:
  0.0 142.7 jit_solution(4348493984897170729)
XLA Ops:
  1.9 136.8 %shard_map.112 = (bf16[128,3584]{1,0:T(8,128)(2,1)}, bf16[128,1536]{1,0:T(8,128)(2,1)}, bf16[128,3584]{1,0:T(8,128)(2,1)}) custom-call(s32[1,128]{1,0:T(1,128)} %bitcast.11, s32[1,128]{1,0:T(1,128)} %bitcast.10, s32[128]{0:T(128)} %store_flat_hbm.1, s32[1]{0:T(128)S(6)} %copy.15.blk_hbm, s32[1]{0:T(128)S(6)} %copy.16.live_hbm, bf16[128,1536]{1,0:T(8,128)(2,1)} %dec_hbm.1, ...), custom_call_target="tpu_custom_call" | custom-call | tf_op jit(solution)/shard_map/pallas_call | solution.py:449
  138.7 0.0 copy-start.1
  138.7 0.0 copy-start
  138.7 2.3 %copy.17 = bf16[128,3584]{1,0:T(8,128)(2,1)} copy(bf16[128,3584]{1,0:T(8,128)(2,1)} %get-tuple-element.12) | data formatting | bytes 1835008
  141.0 0.0 copy-done.1
  141.0 0.7 copy.18
  141.7 0.0 copy-done
  141.7 0.9 copy.19
Async XLA Ops:
  138.7 2.3 %copy-start.1 = (bf16[128,1536]{1,0:T(8,128)(2,1)S(1)}, bf16[128,1536]{1,0:T(8,128)(2,1)}, u32[]{:S(2)}) copy-start(bf16[128,1536]{1,0:T(8,128)(2,1)} %get-tuple-element.7) | copy-start | bytes 1179652
  138.7 3.0 %copy-start = (bf16[128,3584]{1,0:T(8,128)(2,1)S(1)}, bf16[128,3584]{1,0:T(8,128)(2,1)}, u32[]{:S(2)}) copy-start(bf16[128,3584]{1,0:T(8,128)(2,1)} %get-tuple-element.8) | copy-start | bytes 2752516

commit v3 on v2

--- a/solution.py
+++ b/solution.py
@@ -12,6 +12,9 @@
 DEPTH = 4
 CHUNKS = 4
 BLOCK = DEPTH * CHUNKS
+KEPT = 12
+SPARE = 8
+MOVES = ((1, 11), (-1, 10), (-1, 11), (1, 10), (1, 9), (-1, 8))
 MESH = pl.DeviceIdType.MESH
 F32, BF16, I32 = jnp.float32, jnp.bfloat16, jnp.int32
 
@@ -47,6 +50,7 @@
     delta_out,
     down_out,
     up_out,
+    flag_out,
     dec_index_ref,
     store_ref,
     store_s_ref,
@@ -67,7 +71,25 @@
     lpart,
     lpart_got,
     dsend,
-    dgot,
+    xgot,
+    rmeta2,
+    rmeta_send,
+    rmeta_got,
+    t_slot,
+    t_plus,
+    t_minus,
+    t_in,
+    asend,
+    agot,
+    bsend,
+    bgot,
+    spill,
+    fsend,
+    fgot,
+    flag_send,
+    flag_got,
+    flagx_send,
+    flagx_got,
     total,
     load_sems,
     send_sem,
@@ -78,8 +100,17 @@
     part_got_sems,
     lpart_send_sem,
     lpart_got_sem,
-    dsend_sem,
-    dgot_sems,
+    xsend_sem,
+    xgot_sems,
+    rmeta_send_sem,
+    rmeta_got_sem,
+    asend_sem,
+    agot_sems,
+    bsend_sem,
+    bgot_sems,
+    fsend_sem,
+    fgot_sem,
+    flag_sems,
 ):
     zs, xs, ts, shrink, expand = geometry
     owners = zs * xs
@@ -103,9 +134,14 @@
         dz, dx = offset(i)
         return ((z + dz) % zs) * xs + (x + dx) % xs
 
-    def source_of(i):
-        dz, dx = offset(i)
-        return ((z + zs - dz) % zs) * xs + (x + xs - dx) % xs
+    def x_peer(dx):
+        return z * xs + (x + dx) % xs
+
+    def z_peer(dz):
+        return ((z + dz) % zs) * xs + x
+
+    def flow_step(f):
+        return offset(f * xs)[0]
 
     def load(k, src, dst):
         return pltpu.make_async_copy(src, dst, load_sems.at[k])
@@ -227,6 +263,110 @@
 
     lax.fori_loop(1, groups, dispatch_more, 0)
 
+    step = dz
+    flow = block // xs
+    earlier = jnp.logical_or(
+        block_cols < block_rows,
+        jnp.logical_and(block_cols == block_rows, iota(square, 0) < iota(square, 1)),
+    )
+    mates = jnp.logical_and(block_cols // xs == block_rows // xs, earlier)
+    queue = jnp.sum(mates.astype(F32), axis=0, keepdims=True).astype(I32)
+    more = jnp.transpose(jnp.broadcast_to(step * 8 + before, square).astype(F32)).astype(I32)
+    step_col, slot_col = more[:, 0:1] // 8, more[:, 0:1] % 8
+    ring = iota((count, 128), 1) % zs
+    load_of = jnp.sum((ring == step_col).astype(F32), axis=0, keepdims=True)
+
+    def from_next(v):
+        return pltpu.roll(v, 127, 1)
+
+    def from_last(v):
+        return pltpu.roll(v, 1, 1)
+
+    load_of = jnp.broadcast_to(load_of, (8, 128))
+    above, below = from_next(load_of), from_last(load_of)
+    rest = jnp.maximum(load_of - KEPT, 0.0)
+    moved = []
+    for way, top in MOVES:
+        can = ((above if way > 0 else below) <= top).astype(F32)
+        if len(moved) == 2:
+            can = can * (1.0 - from_last(from_last(moved[0])))
+        if len(moved) == 3:
+            can = can * (1.0 - from_next(from_next(moved[1])))
+        now = jnp.where(rest > 0, can, 0.0)
+        rest = rest - now
+        moved.append(now)
+    stuck = jnp.max(rest, axis=1, keepdims=True)
+    row8 = iota((8, 128), 0)
+    leave = jnp.zeros((8, 128), F32)
+    enter = jnp.zeros((8, 128), F32)
+    for m, (way, _) in enumerate(MOVES):
+        leave = jnp.where(row8 == m, moved[m], leave)
+        enter = jnp.where(row8 == m, from_last(moved[m]) if way > 0 else from_next(moved[m]), enter)
+    at_step = (iota((128, count), 0) == step).astype(F32).astype(BF16)
+    mine = nn_dot(leave.astype(BF16), at_step)
+    code = jnp.where(queue < KEPT, queue + 1, 0)
+    home_step, home_slot = step, queue
+    seen = jnp.zeros((1, count), F32)
+    over = (queue - KEPT).astype(F32)
+    for m, (way, top) in enumerate(MOVES):
+        used = mine[m : m + 1]
+        hit = jnp.where(over == seen, used, 0.0) > 0.5
+        code = jnp.where(hit, KEPT + 1 + m, code)
+        home_step = jnp.where(hit, (step + zs + way) % zs, home_step)
+        home_slot = jnp.where(hit, top, home_slot)
+        seen = seen + used
+    home_far = (home_step >= zs // 2).astype(I32)
+    home_k = jnp.where(
+        home_step < zs // 2, home_step, jnp.where(home_step == zs // 2, 0, zs - home_step)
+    )
+    home = jnp.where(code > 0, (2 * home_k + home_far) * 16 + home_slot, 4095)
+    home_cols = jnp.transpose(jnp.broadcast_to(home, square).astype(F32)).astype(I32)[:, 0:1]
+    code_col = jnp.transpose(jnp.broadcast_to(code, square).astype(F32))[:, 0:1]
+    block_col = block_cols[:, 0:1]
+    lane_x = lanes // BLOCK
+    lane_r = lanes % DEPTH
+    fits = jnp.logical_and(lane_x == block_col % xs, lane_r == slot_col)
+    codes = jnp.where(fits, jnp.broadcast_to(code_col, (count, 128)), 0.0).astype(BF16)
+    in_flow = (iota((zs, count), 0) == flow).astype(F32).astype(BF16)
+    signs = jnp.concatenate(
+        [
+            jnp.zeros((64, 128), F32),
+            leave,
+            enter,
+            jnp.broadcast_to(stuck, (8, 128)),
+            jnp.zeros((40, 128), F32),
+        ],
+        axis=0,
+    )
+    signs = jnp.transpose(signs).astype(BF16)
+    fi = iota((zs, 128), 0)
+    f_near = fi // 2
+    f_step = jnp.where(
+        fi % 2 == 0, f_near, jnp.where(f_near == 0, zs // 2, zs - f_near)
+    )
+    pick = (f_step == iota((zs, 128), 1)).astype(F32).astype(BF16)
+    rmeta2[...] = nn_dot(in_flow, codes) + nn_dot(pick, signs)
+
+    def lift_plan(f, carry):
+        rmeta_send[f] = rmeta2[pl.ds(f, 1), :]
+        return carry
+
+    lax.fori_loop(0, zs, lift_plan, 0)
+    rmeta_got[0] = rmeta2[0:1, :]
+
+    def start_plan(f, carry):
+        pltpu.make_async_remote_copy(
+            src_ref=rmeta_send.at[f],
+            dst_ref=rmeta_got.at[f],
+            send_sem=rmeta_send_sem,
+            recv_sem=rmeta_got_sem,
+            device_id=(z_peer(flow_step(f)), t),
+            device_id_type=MESH,
+        ).start()
+        return carry
+
+    lax.fori_loop(1, zs, start_plan, 0)
+
     rank = down.shape[0] // 2
     learn = rows.shape[0]
     own_slot = store_s_ref[blk_s_ref[0]] % 2
@@ -318,20 +458,22 @@
 
         lax.fori_loop(1, ts, start, 0)
 
-    def delta_copy(i):
-        at = pl.ds(pl.multiple_of(i * BLOCK, BLOCK), BLOCK)
-        return pltpu.make_async_remote_copy(
-            src_ref=dsend.at[at],
-            dst_ref=dgot.at[at],
-            send_sem=dsend_sem,
-            recv_sem=dgot_sems.at[i // wide],
-            device_id=(source_of(i), t),
-            device_id_type=MESH,
-        )
-
-    def start_delta(i, carry):
-        delta_copy(i).start()
-        return carry
+    def start_cross(g):
+        for half in range(2):
+            for dx in range(xs):
+                row = (g * wide + half * xs + dx) * BLOCK
+                at = pl.ds(pl.multiple_of(row, BLOCK), BLOCK)
+                if dx == 0:
+                    pltpu.make_async_copy(dsend.at[at], xgot.at[at], xgot_sems.at[g]).start()
+                else:
+                    pltpu.make_async_remote_copy(
+                        src_ref=dsend.at[at],
+                        dst_ref=xgot.at[at],
+                        send_sem=xsend_sem,
+                        recv_sem=xgot_sems.at[g],
+                        device_id=(x_peer(xs - dx), t),
+                        device_id_type=MESH,
+                    ).start()
 
     def deltas(g):
         view = part_got.at[g]
@@ -355,24 +497,172 @@
             sum_rows += nn_dot(left, up[:, c * hc : (c + 1) * hc])
         dsend[pl.ds(base, gr), :] = (sum_rows * expand).astype(BF16)
 
+        start_cross(g)
+
+    def read_plans():
+        view = rmeta_got.at[pl.ds(1, zs - 1)]
+        pltpu.make_async_copy(view, view, rmeta_got_sem).wait()
+        plan = rmeta_got[...].reshape(zs, 128)
+        lane16 = iota((zs, 128), 1)
+        source = (z + zs - f_step) % zs
+        other_f = iota((zs, zs), 1)
+        other_near = other_f // 2
+        other_step = jnp.where(
+            other_f % 2 == 0, other_near, jnp.where(other_near == 0, zs // 2, zs - other_near)
+        )
+        other = (z + zs - other_step) % zs
+        first = (other < source[:, 0:1]).astype(F32).astype(BF16)
+        ahead = nn_dot(first, plan.astype(BF16))
+
+        def column(v, n):
+            return jnp.sum(jnp.where(lane16 == n, v, 0.0), axis=1, keepdims=True)
+
+        def places(base, order):
+            here = [column(plan, base + m) for m in order]
+            at = column(ahead, base + order[0])
+            for m in order[1:]:
+                at = at + column(ahead, base + m)
+            out = []
+            for one in here:
+                out.append(jnp.where(one > 0.5, at, -1.0))
+                at = at + one
+            return out, at
+
+        ups = [m for m, (way, _) in enumerate(MOVES) if way > 0]
+        downs = [m for m, (way, _) in enumerate(MOVES) if way < 0]
+        t_slot[...] = jnp.where(plan < KEPT + 0.5, plan - 1.0, -1.0)
+        worst = column(plan, 80)
+        for table, order in ((t_plus, ups), (t_minus, downs)):
+            spots, end = places(64, order)
+            worst = jnp.maximum(worst, jnp.where(end > SPARE + 0.5, 1.0, 0.0))
+            value = jnp.full((zs, 128), -1.0, F32)
+            for m, spot in zip(order, spots):
+                value = jnp.where(plan == KEPT + 1.0 + m, spot, value)
+            table[...] = value
+        value = jnp.full((zs, 128), -1.0, F32)
+        spot_lane = (lane16 % SPARE).astype(F32)
+        side_lane = lane16 // (SPARE * CHUNKS)
+        for side, order in ((0, ups), (1, downs)):
+            spots, _ = places(72, order)
+            for m, spot in zip(order, spots):
+                hit = jnp.logical_and(side_lane == side, spot_lane == spot)
+                value = jnp.where(hit, MOVES[m][1] - 8.0, value)
+        t_in[...] = value
+        worst = jnp.max(worst, axis=0, keepdims=True)
+        flag_send[...] = jnp.broadcast_to(worst, (1, 128))
+        flag_got[0] = flag_send[...]
+
+        def start(f, carry):
+            pltpu.make_async_remote_copy(
+                src_ref=flag_send,
+                dst_ref=flag_got.at[f],
+                send_sem=flag_sems.at[0],
+                recv_sem=flag_sems.at[1],
+                device_id=(z_peer(flow_step(f)), t),
+                device_id_type=MESH,
+            ).start()
+            return carry
+
+        lax.fori_loop(1, zs, start, 0)
+        spill[...] = jnp.zeros_like(spill)
+
+    def pick_rows(table, f, per, cells):
+        shape = (per * CHUNKS, cells)
+        wanted = (iota(shape, 0) % per).astype(F32)
+        here = jnp.broadcast_to(table[pl.ds(f, 1), :][:, :cells], shape)
+        return here, wanted, iota(shape, 0) // per
+
+    cells = xs * BLOCK
+    kept_a, kept_b = 8 * CHUNKS, DEPTH * CHUNKS
+
+    def a_copy(f):
+        at = pl.ds(pl.multiple_of(f * kept_a, kept_a), kept_a)
+        return pltpu.make_async_remote_copy(
+            src_ref=asend.at[at],
+            dst_ref=agot.at[at],
+            send_sem=asend_sem,
+            recv_sem=agot_sems.at[f // 2],
+            device_id=(z_peer(zs - flow_step(f)), t),
+            device_id_type=MESH,
+        )
+
+    def start_a(f, carry):
+        a_copy(f).start()
+        return carry
+
+    held_back = min(3, groups - 1)
+
+    def relay(g):
+        view = xgot.at[pl.ds(pl.multiple_of(g * gr, gr), gr)]
+        pltpu.make_async_copy(view, view, xgot_sems.at[g]).wait()
+
+        def one_flow(f, carry):
+            chunk = (iota((1, cells), 1) % BLOCK) // DEPTH
+            picks = []
+            for table, per, base in (
+                (t_slot, 8, 0.0),
+                (t_slot, DEPTH, 8.0),
+                (t_plus, SPARE, 0.0),
+                (t_minus, SPARE, 0.0),
+            ):
+                here, wanted, c = pick_rows(table, f, per, cells)
+                hit = jnp.logical_and(here == wanted + base, chunk == c)
+                picks.append(hit.astype(F32))
+            picks = jnp.concatenate(picks, axis=0).astype(BF16)
+            blocks = xgot[pl.ds(pl.multiple_of(f * cells, cells), cells), :]
+            packed = nn_dot(picks, blocks)
+            asend[pl.ds(pl.multiple_of(f * kept_a, kept_a), kept_a), :] = packed[:kept_a].astype(BF16)
+            bsend[pl.ds(pl.multiple_of(f * kept_b, kept_b), kept_b), :] = packed[
+                kept_a : kept_a + kept_b
+            ].astype(BF16)
+            spill[...] += packed[kept_a + kept_b :]
+            return carry
+
+        lax.fori_loop(2 * g, 2 * g + 2, one_flow, 0)
+
         @pl.when(g == 0)
         def _():
-            dgot[0:BLOCK, :] = dsend[0:BLOCK, :]
-            lax.fori_loop(1, wide, start_delta, 0)
-
-        @pl.when(g > 0)
+            agot[0:kept_a, :] = asend[0:kept_a, :]
+            lax.fori_loop(1, 2, start_a, 0)
+
+        @pl.when(jnp.logical_and(g > 0, g < groups - held_back))
         def _():
-            lax.fori_loop(g * wide, (g + 1) * wide, start_delta, 0)
-
-    ranks(0)
-
-    def step(g, carry):
-        ranks(g)
-        deltas(g - 1)
-        return carry
-
-    lax.fori_loop(1, groups, step, 0)
-    deltas(groups - 1)
+            lax.fori_loop(2 * g, 2 * g + 2, start_a, 0)
+
+    def stage(s, carry):
+        @pl.when(s < groups)
+        def _():
+            ranks(s)
+
+        @pl.when(s == 1)
+        def _():
+            read_plans()
+
+        @pl.when(jnp.logical_and(s >= 1, s < groups + 1))
+        def _():
+            deltas(s - 1)
+
+        @pl.when(s >= 2)
+        def _():
+            relay(s - 2)
+
+        return carry
+
+    lax.fori_loop(0, groups + 2, stage, 0)
+
+    spare = SPARE * CHUNKS
+    fsend[...] = spill[...].astype(BF16)
+    for side, way in ((0, 1), (1, zs - 1)):
+        at = pl.ds(side * spare, spare)
+        pltpu.make_async_remote_copy(
+            src_ref=fsend.at[at],
+            dst_ref=fgot.at[at],
+            send_sem=fsend_sem,
+            recv_sem=fgot_sem,
+            device_id=(z_peer(way), t),
+            device_id_type=MESH,
+        ).start()
+    lax.fori_loop(2 * (groups - held_back), 2 * groups, start_a, 0)
 
     pltpu.make_async_copy(lpart_got, lpart_got, lpart_got_sem).wait()
     v = lpart[...]
@@ -393,30 +683,180 @@
         g_b = tn_dot(act, grad[:, at]) * expand
         up_out[:, at] = (up[:, at].astype(F32) - UP_RATE * g_b).astype(BF16)
 
+    pltpu.make_async_copy(fgot, fgot, fgot_sem).wait()
+
+    def b_copy(f):
+        at = pl.ds(pl.multiple_of(f * kept_b, kept_b), kept_b)
+        return pltpu.make_async_remote_copy(
+            src_ref=bsend.at[at],
+            dst_ref=bgot.at[at],
+            send_sem=bsend_sem,
+            recv_sem=bgot_sems.at[f // 4],
+            device_id=(z_peer(zs - flow_step(f)), t),
+            device_id_type=MESH,
+        )
+
+    def finish_b(f, carry):
+        here, wanted, c = pick_rows(t_in, f, DEPTH, 2 * spare)
+        chunk = (iota((1, 2 * spare), 1) % spare) // SPARE
+        hit = jnp.logical_and(here == wanted, chunk == c)
+        at = pl.ds(pl.multiple_of(f * kept_b, kept_b), kept_b)
+        extra = nn_dot(hit.astype(F32).astype(BF16), fgot[...])
+        bsend[at, :] = (bsend[at, :].astype(F32) + extra).astype(BF16)
+
+        @pl.when(f > 0)
+        def _():
+            b_copy(f).start()
+
+        return carry
+
+    lax.fori_loop(0, zs, finish_b, 0)
+    bgot[0:kept_b, :] = bsend[0:kept_b, :]
+
+    pltpu.make_async_copy(
+        flag_got.at[pl.ds(1, zs - 1)], flag_got.at[pl.ds(1, zs - 1)], flag_sems.at[1]
+    ).wait()
+    worst = flag_got[0]
+    for f in range(1, zs):
+        worst = jnp.maximum(worst, flag_got[f])
+    flagx_send[...] = worst
+    for dx in range(1, xs):
+        pltpu.make_async_remote_copy(
+            src_ref=flagx_send,
+            dst_ref=flagx_got.at[dx - 1],
+            send_sem=flag_sems.at[2],
+            recv_sem=flag_sems.at[3],
+            device_id=(x_peer(dx), t),
+            device_id_type=MESH,
+        ).start()
+
     total[...] = jnp.zeros_like(total)
-    place_128 = jnp.broadcast_to(place_cols[:, 0:1], (count, gr))
-
-    def combine(g, carry):
-        wait_group(g, dgot, BLOCK, dgot_sems)
-        base = pl.multiple_of(g * gr, gr)
-        rel = iota((count, gr), 1) + base
-        arrived = dgot[pl.ds(base, gr), :]
+    pair = 2 * kept_a
+    home_flow = jnp.broadcast_to(home_cols // 16, (count, pair))
+    home_slot = jnp.broadcast_to(home_cols % 16, (count, pair))
+    in_a = home_slot < 8
+    place_a = jnp.where(in_a, home_flow * kept_a + home_slot, -4096)
+    place_b = jnp.where(in_a, -4096, home_flow * kept_b + home_slot - 8)
+
+    def add_up(ref, g, place, chunk_rows):
+        base = pl.multiple_of(g * pair, pair)
+        rel = iota((count, pair), 1) + base
+        arrived = ref[pl.ds(base, pair), :]
         for c in range(CHUNKS):
-            chosen = (rel == place_128 + c * DEPTH).astype(F32).astype(BF16)
+            chosen = (rel == place + c * chunk_rows).astype(F32).astype(BF16)
             total[:, c * hc : (c + 1) * hc] += nn_dot(chosen, arrived)
-        return carry
-
-    lax.fori_loop(0, groups, combine, 0)
+
+    def wait_pair(ref, g, own, sems):
+        @pl.when(g == 0)
+        def _():
+            view = ref.at[pl.ds(own, pair - own)]
+            pltpu.make_async_copy(view, view, sems.at[g]).wait()
+
+        @pl.when(g > 0)
+        def _():
+            view = ref.at[pl.ds(pl.multiple_of(g * pair, pair), pair)]
+            pltpu.make_async_copy(view, view, sems.at[g]).wait()
+
+    def combine_a(g, carry):
+        wait_pair(agot, g, kept_a, agot_sems)
+        add_up(agot, g, place_a, 8)
+        return carry
+
+    lax.fori_loop(0, groups, combine_a, 0)
+
+    def combine_b(g, carry):
+        wait_pair(bgot, g, kept_b, bgot_sems)
+        add_up(bgot, g, place_b, DEPTH)
+        return carry
+
+    lax.fori_loop(0, zs // 4, combine_b, 0)
     delta_out[...] = total[...].astype(BF16)
+    pltpu.make_async_copy(flagx_got, flagx_got, flag_sems.at[3]).wait()
+    worst = flagx_send[...]
+    for dx in range(1, xs):
+        worst = jnp.maximum(worst, flagx_got[dx - 1])
+    flag_out[...] = jnp.broadcast_to(worst, (8, 128))
 
     def drain(view, sem):
         pltpu.make_async_copy(view, view, sem).wait()
 
     drain(send.at[pl.ds(BLOCK, (owners - 1) * BLOCK)], send_sem)
     drain(meta_send.at[pl.ds(1, owners - 1)], meta_send_sem)
-    drain(dsend.at[pl.ds(BLOCK, (owners - 1) * BLOCK)], dsend_sem)
+    drain(dsend.at[pl.ds(0, zs * (xs - 1) * BLOCK)], xsend_sem)
+    drain(rmeta_send.at[pl.ds(1, zs - 1)], rmeta_send_sem)
+    drain(asend.at[pl.ds(kept_a, (zs - 1) * kept_a)], asend_sem)
+    drain(bsend.at[pl.ds(kept_b, (zs - 1) * kept_b)], bsend_sem)
+    drain(fsend, fsend_sem)
+    drain(flag_got.at[pl.ds(1, zs - 1)], flag_sems.at[0])
+    drain(flagx_got, flag_sems.at[2])
     drain(lpart_got, lpart_send_sem)
     drain(part_got, part_send_sem)
+
+
+def lookup(table, wanted):
+    hits = wanted[:, None] == jnp.arange(table.shape[0], dtype=jnp.int32)[None, :]
+    return jnp.sum(jnp.where(hits, table[None, :], 0), axis=1)
+
+
+def padded_exchange(
+    decode_input_rows,
+    decode_adapter_index,
+    adapter_storage_index,
+    adapter_down_weight,
+    adapter_up_weight,
+):
+    owners = lax.axis_size("dp")
+    split_points = lax.axis_size("tensor")
+    holder_mask, rank_extent, width_portion = adapter_down_weight.shape
+    hidden_portion = adapter_up_weight.shape[2]
+    shrink = (width_portion * split_points) ** (-0.5)
+    expand = rank_extent ** (-0.5)
+    row_count = decode_input_rows.shape[0]
+    slot_depth = 2 * row_count // owners
+    total_slots = owners * slot_depth
+    slot_row = lookup(adapter_storage_index, decode_adapter_index)
+    target = slot_row // holder_mask
+    local_slot = slot_row % holder_mask
+    target_hot = (target[:, None] == jnp.arange(owners, dtype=jnp.int32)[None, :]).astype(jnp.int32)
+    before = jnp.cumsum(target_hot, axis=0) - target_hot
+    position = target * slot_depth + jnp.sum(before * target_hot, axis=1)
+    matches = jnp.arange(total_slots, dtype=jnp.int32)[:, None] == position[None, :]
+    dispatch = matches.astype(jnp.bfloat16)
+    send_rows = jnp.dot(dispatch, decode_input_rows, preferred_element_type=jnp.float32).astype(
+        jnp.bfloat16
+    )
+    filled = jnp.any(matches, axis=1)
+    send_local = jnp.where(filled, jnp.sum(jnp.where(matches, local_slot[None, :], 0), axis=1), -1)
+    send_rows = send_rows.reshape(owners, slot_depth, width_portion)
+    send_local = send_local.astype(jnp.bfloat16).reshape(owners, slot_depth)
+    flattened_second = adapter_up_weight.reshape(holder_mask * rank_extent, hidden_portion)
+    got_rows, got_local = (
+        lax.all_to_all(send_rows, "dp", split_axis=0, concat_axis=0, tiled=True),
+        lax.all_to_all(send_local, "dp", split_axis=0, concat_axis=0, tiled=True),
+    )
+    sources, items = got_local.shape
+    flattened_rows = got_rows.reshape(sources * items, width_portion)
+    which_slot = got_local.reshape(-1).astype(jnp.float32)
+    chosen = (which_slot[:, None] == jnp.arange(holder_mask, dtype=jnp.float32)[None, :]).astype(
+        jnp.float32
+    )
+    partial_output = jnp.einsum(
+        "lm,kjm->lkj", flattened_rows, adapter_down_weight, preferred_element_type=jnp.float32
+    )
+    to_sum = partial_output.reshape(sources * items, holder_mask * rank_extent)
+    summed = lax.psum(to_sum, "tensor")
+    spread = summed.reshape(sources * items, holder_mask, rank_extent) * chosen[:, :, None]
+    hidden = (
+        (spread * shrink).reshape(sources * items, holder_mask * rank_extent).astype(jnp.bfloat16)
+    )
+    delta_rows = jnp.dot(hidden, flattened_second, preferred_element_type=jnp.float32) * expand
+    answer = delta_rows.astype(jnp.bfloat16).reshape(sources, items, hidden_portion)
+    returned = lax.all_to_all(answer, "dp", split_axis=0, concat_axis=0, tiled=True)
+    merged = returned.reshape(total_slots, hidden_portion)
+    dec_delta = jnp.einsum(
+        "mr,mf->rf", dispatch, merged, preferred_element_type=jnp.float32
+    ).astype(jnp.bfloat16)
+    return dec_delta
 
 
 def local(
@@ -446,15 +886,18 @@
     hbm = pl.BlockSpec(memory_space=pltpu.HBM)
     dma = pltpu.SemaphoreType.DMA
     packed = (wide // 4, 8, 2 * rank)
-    delta, down, up = pl.pallas_call(
+    rows_a, rows_b, spare = 8 * CHUNKS, DEPTH * CHUNKS, SPARE * CHUNKS
+    chunk = hidden // CHUNKS
+    delta, down, up, flag = pl.pallas_call(
         functools.partial(kernel, (zs, xs, ts, shrink, expand)),
         out_shape=(
             jax.ShapeDtypeStruct((count, hidden), BF16),
             jax.ShapeDtypeStruct((held * rank, width), BF16),
             jax.ShapeDtypeStruct((held * rank, hidden), BF16),
+            jax.ShapeDtypeStruct((8, 128), F32),
         ),
         in_specs=[hbm] * 10,
-        out_specs=(vmem, vmem, vmem),
+        out_specs=(vmem, vmem, vmem, vmem),
         scratch_shapes=[
             pltpu.VMEM((1, count), I32),
             pltpu.VMEM((1, adapter_storage_index.shape[0]), I32),
@@ -475,8 +918,26 @@
             pltpu.VMEM((groups, ts - 1) + packed, F32),
             pltpu.VMEM((learn, 2 * rank), F32),
             pltpu.VMEM((ts - 1, learn, 2 * rank), F32),
-            pltpu.VMEM((owners * BLOCK, hidden // CHUNKS), BF16),
-            pltpu.VMEM((owners * BLOCK, hidden // CHUNKS), BF16),
+            pltpu.VMEM((owners * BLOCK, chunk), BF16),
+            pltpu.VMEM((owners * BLOCK, chunk), BF16),
+            pltpu.VMEM((zs, 128), F32),
+            pltpu.VMEM((zs, 1, 128), F32),
+            pltpu.VMEM((zs, 1, 128), F32),
+            pltpu.VMEM((zs, 128), F32),
+            pltpu.VMEM((zs, 128), F32),
+            pltpu.VMEM((zs, 128), F32),
+            pltpu.VMEM((zs, 128), F32),
+            pltpu.VMEM((zs * rows_a, chunk), BF16),
+            pltpu.VMEM((zs * rows_a, chunk), BF16),
+            pltpu.VMEM((zs * rows_b, chunk), BF16),
+            pltpu.VMEM((zs * rows_b, chunk), BF16),
+            pltpu.VMEM((2 * spare, chunk), F32),
+            pltpu.VMEM((2 * spare, chunk), BF16),
+            pltpu.VMEM((2 * spare, chunk), BF16),
+            pltpu.VMEM((1, 128), F32),
+            pltpu.VMEM((zs, 1, 128), F32),
+            pltpu.VMEM((1, 128), F32),
+            pltpu.VMEM((xs - 1, 1, 128), F32),
             pltpu.VMEM((count, hidden), F32),
             dma((10,)),
             dma,
@@ -489,6 +950,15 @@
             dma,
             dma,
             dma((groups,)),
+            dma,
+            dma,
+            dma,
+            dma((groups,)),
+            dma,
+            dma((zs // 4,)),
+            dma,
+            dma,
+            dma((4,)),
         ],
         compiler_params=pltpu.CompilerParams(
             collective_id=0, has_side_effects=True, vmem_limit_bytes=58 * 1024 * 1024
@@ -505,6 +975,16 @@
         adapter_down_weight.reshape(held * rank, width),
         adapter_up_weight.reshape(held * rank, hidden),
     )
+    def padded():
+        return padded_exchange(
+            decode_input_rows,
+            decode_adapter_index,
+            adapter_storage_index,
+            adapter_down_weight,
+            adapter_up_weight,
+        )
+
+    delta = lax.cond(flag[0, 0] > 0.5, padded, lambda: delta)
     return delta, down.reshape(held, rank, width), up.reshape(held, rank, hidden)
 
 

time: 145 us -> 160 us (1.10)
  between operations: 1.95 us -> 16.2 us
    unnamed x7 -> x17, local copies, waits for them, and re-layouts: 3.94 us -> 3.96 us
where the time goes in v3:
time: 160 us; the launch traced here: 157 us
  Pallas kernels  136 us (85%)
  between operations  16.2 us (10%)
  local copies, waits for them, and re-layouts  5.15 us (3%)
    pallas_call x1, Pallas kernels, local(): pl.pallas_call(functools.partial(kernel, (zs, xs, ts, shrink, expand)), o...  136 us
    unnamed x17, local copies, waits for them, and re-layouts  3.96 us

profile of v3, /device:TPU:24, one launch (start us, length us, event | category | flops | bytes accessed | tf_op | source)
XLA Modules:
  0.0 157.5 jit_solution(4834556620011906955)
XLA Ops:
  7.2 0.0 copy-start.5
  7.2 0.0 copy-start
  7.2 0.0 copy-start.2
  7.2 0.0 copy-start.6
  7.2 0.0 copy-start.1
  8.6 136.1 %shard_map.112 = (bf16[128,3584]{1,0:T(8,128)(2,1)}, bf16[128,1536]{1,0:T(8,128)(2,1)}, bf16[128,3584]{1,0:T(8,128)(2,1)}, f32[8,128]{1,0:T(8,128)}) custom-call(s32[1,128]{1,0:T(1,128)} %bitcast.23, s32[1,128]{1,0:T(1,128)} %bitcast.22, s32[128]{0:T(128)} %store_flat_hbm.1, s32[1]{0:T(128)S(6)} %copy.22.blk_hbm, s32[1]{0:T(128)S(6)} %copy.23.live_hbm, ...), custom_call_target="tpu_custom_call" | custom-call | tf_op jit(solution)/shard_map/pallas_call | solution.py:891
  144.8 1.2 slice.3
  146.6 0.0 copy-done.5
  146.6 0.0 copy-done
  146.6 0.0 copy-done.2
  146.6 0.0 copy-done.6
  146.6 0.0 copy-done.1
  146.7 0.0 copy-start.4
  146.7 0.0 copy-start.3
  146.7 2.3 %copy.24 = bf16[128,3584]{1,0:T(8,128)(2,1)} copy(bf16[128,3584]{1,0:T(8,128)(2,1)} %get-tuple-element.38) | data formatting | bytes 1835008
  148.9 0.0 copy-done.4
  148.9 0.7 copy.25
  149.7 0.0 copy-done.3
  149.7 0.9 copy.26
  (1 shorter events, 0.0 us)
Async XLA Ops:
  7.2 139.4 %copy-start.5 = (s32[128]{0:T(128)S(1)}, s32[128]{0:T(128)}, u32[]{:S(2)}) copy-start(s32[128]{0:T(128)} %store_flat_hbm.1) | copy-start | bytes 1540
  7.2 139.4 %copy-start = (bf16[2,64,3584]{2,1,0:T(8,128)(2,1)S(1)}, bf16[2,64,3584]{2,1,0:T(8,128)(2,1)}, u32[]{:S(2)}) copy-start(bf16[2,64,3584]{2,1,0:T(8,128)(2,1)} %param.19) | copy-start | bytes 2752516
  7.2 139.4 %copy-start.2 = (bf16[2,64,1536]{2,1,0:T(8,128)(2,1)S(1)}, bf16[2,64,1536]{2,1,0:T(8,128)(2,1)}, u32[]{:S(2)}) copy-start(bf16[2,64,1536]{2,1,0:T(8,128)(2,1)} %param.18) | copy-start | bytes 1179652
  7.2 139.4 %copy-start.6 = (s32[128]{0:T(128)S(1)}, s32[128]{0:T(128)}, u32[]{:S(2)}) copy-start(s32[128]{0:T(128)} %param.12) | copy-start | bytes 1540
  7.2 139.4 %copy-start.1 = (bf16[128,1536]{1,0:T(8,128)(2,1)S(1)}, bf16[128,1536]{1,0:T(8,128)(2,1)}, u32[]{:S(2)}) copy-start(bf16[128,1536]{1,0:T(8,128)(2,1)} %dec_hbm.1) | copy-start | bytes 1179652
  146.7 2.3 %copy-start.4 = (bf16[128,1536]{1,0:T(8,128)(2,1)S(1)}, bf16[128,1536]{1,0:T(8,128)(2,1)}, u32[]{:S(2)}) copy-start(bf16[128,1536]{1,0:T(8,128)(2,1)} %get-tuple-element.28) | copy-start | bytes 1179652
  146.7 3.0 %copy-start.3 = (bf16[128,3584]{1,0:T(8,128)(2,1)S(1)}, bf16[128,3584]{1,0:T(8,128)(2,1)}, u32[]{:S(2)}) copy-start(bf16[128,3584]{1,0:T(8,128)(2,1)} %get-tuple-element.29) | copy-start | bytes 2752516

commit v4 on v3

--- a/solution.py
+++ b/solution.py
@@ -15,6 +15,7 @@
 KEPT = 12
 SPARE = 8
 MOVES = ((1, 11), (-1, 10), (-1, 11), (1, 10), (1, 9), (-1, 8))
+VMEM_LIMIT = 58 * 1024 * 1024
 MESH = pl.DeviceIdType.MESH
 F32, BF16, I32 = jnp.float32, jnp.bfloat16, jnp.int32
 
@@ -119,29 +120,30 @@
     gr = wide * BLOCK
     me = lax.axis_index("dp")
     t = lax.axis_index("tensor")
-    z, x = me // xs, me % xs
+    z, x = lax.div(me, xs), lax.rem(me, xs)
     count = dec.shape[0]
     wc = dec.shape[1] // CHUNKS
     hc = grad.shape[1] // CHUNKS
 
-    def offset(i):
-        k = i // wide
-        half = (i % wide) // xs
-        dz = k + half * (zs - 2 * k - (zs // 2) * ((zs - k) // zs))
-        return dz, i % xs
-
-    def owner_of(i):
-        dz, dx = offset(i)
-        return ((z + dz) % zs) * xs + (x + dx) % xs
+    x_at = [lax.rem(x + dx, xs) for dx in range(xs)]
+    t_at = [lax.rem(t + j, ts) for j in range(ts)]
+
+    def flow_step(f):
+        near = lax.rem(zs // 2 - lax.div(f, 2), zs // 2)
+        return near + lax.rem(f, 2) * (zs - 2 * near - (zs // 2) * lax.div(zs - near, zs))
 
     def x_peer(dx):
-        return z * xs + (x + dx) % xs
+        return z * xs + x_at[dx]
 
     def z_peer(dz):
-        return ((z + dz) % zs) * xs + x
-
-    def flow_step(f):
-        return offset(f * xs)[0]
+        return lax.rem(z + dz, zs) * xs + x
+
+    def z_row(f):
+        return lax.rem(z + flow_step(f), zs) * xs
+
+    def steps_of_flows(f):
+        near = jnp.where(f // 2 == 0, 0, zs // 2 - f // 2)
+        return jnp.where(f % 2 == 0, near, jnp.where(near == 0, zs // 2, zs - near))
 
     def load(k, src, dst):
         return pltpu.make_async_copy(src, dst, load_sems.at[k])
@@ -164,17 +166,22 @@
 
     barrier = pltpu.get_barrier_semaphore()
 
-    def greet(i, carry):
-        pl.semaphore_signal(barrier, inc=1, device_id=(owner_of(i), t), device_id_type=MESH)
-        return carry
-
-    lax.fori_loop(1, owners, greet, 0)
-
-    def greet_t(j, carry):
-        pl.semaphore_signal(barrier, inc=1, device_id=(me, (t + j) % ts), device_id_type=MESH)
-        return carry
-
-    lax.fori_loop(1, ts, greet_t, 0)
+    def greet(f, first):
+        base = z_row(f)
+        for dx in range(first, xs):
+            pl.semaphore_signal(
+                barrier, inc=1, device_id=(base + x_at[dx], t), device_id_type=MESH
+            )
+
+    def greet_flow(f, carry):
+        greet(f, 0)
+        return carry
+
+    greet(0, 1)
+    lax.fori_loop(1, zs, greet_flow, 0)
+
+    for j in range(1, ts):
+        pl.semaphore_signal(barrier, inc=1, device_id=(me, t_at[j]), device_id_type=MESH)
 
     for one in loads[1:6]:
         one.wait()
@@ -188,7 +195,8 @@
     dx = (owner % xs - x + xs) % xs
     half = (dz >= zs // 2).astype(I32)
     k = jnp.where(dz < zs // 2, dz, jnp.where(dz == zs // 2, 0, zs - dz))
-    block = k * wide + half * xs + dx
+    turn = jnp.where(k == 0, 0, zs // 2 - k)
+    block = turn * wide + half * xs + dx
     square = (count, count)
     block_rows = jnp.broadcast_to(block, square)
     block_cols = jnp.transpose(block_rows.astype(F32)).astype(I32)
@@ -217,31 +225,27 @@
     loads[0].wait()
     pl.semaphore_wait(barrier, owners - 1 + ts - 1)
 
-    def row_copy(i):
-        at = pl.ds(pl.multiple_of(i * BLOCK, BLOCK), BLOCK)
-        return pltpu.make_async_remote_copy(
-            src_ref=send.at[at],
-            dst_ref=got.at[at],
-            send_sem=send_sem,
-            recv_sem=got_sems.at[i // wide],
-            device_id=(owner_of(i), t),
-            device_id_type=MESH,
-        )
-
-    def meta_copy(i):
-        return pltpu.make_async_remote_copy(
-            src_ref=meta_send.at[i],
-            dst_ref=meta_got.at[i],
-            send_sem=meta_send_sem,
-            recv_sem=meta_got_sems.at[i // wide],
-            device_id=(owner_of(i), t),
-            device_id_type=MESH,
-        )
-
-    def start_rows(i, carry):
-        meta_copy(i).start()
-        row_copy(i).start()
-        return carry
+    def start_rows(g, first):
+        for half in range(2):
+            base = z_row(2 * g + half)
+            for dx in range(first if half == 0 else 0, xs):
+                i = g * wide + half * xs + dx
+                at = pl.ds(pl.multiple_of(i * BLOCK, BLOCK), BLOCK)
+                to = dict(device_id=(base + x_at[dx], t), device_id_type=MESH)
+                pltpu.make_async_remote_copy(
+                    src_ref=send.at[at],
+                    dst_ref=got.at[at],
+                    send_sem=send_sem,
+                    recv_sem=got_sems.at[g],
+                    **to,
+                ).start()
+                pltpu.make_async_remote_copy(
+                    src_ref=meta_send.at[i],
+                    dst_ref=meta_got.at[i],
+                    send_sem=meta_send_sem,
+                    recv_sem=meta_got_sems.at[g],
+                    **to,
+                ).start()
 
     def dispatch(g):
         base = pl.multiple_of(g * gr, gr)
@@ -253,15 +257,15 @@
         send[pl.ds(base, gr), :] = sum_rows.astype(BF16)
 
     dispatch(0)
-    lax.fori_loop(1, wide, start_rows, 0)
+    start_rows(0, 1)
     got[0:BLOCK, :] = send[0:BLOCK, :]
 
     def dispatch_more(g, carry):
         dispatch(g)
-        lax.fori_loop(g * wide, (g + 1) * wide, start_rows, 0)
-        return carry
-
-    lax.fori_loop(1, groups, dispatch_more, 0)
+        start_rows(g, 0)
+        return carry
+
+    dispatch_more(1, 0)
 
     step = dz
     flow = block // xs
@@ -319,7 +323,8 @@
     home_k = jnp.where(
         home_step < zs // 2, home_step, jnp.where(home_step == zs // 2, 0, zs - home_step)
     )
-    home = jnp.where(code > 0, (2 * home_k + home_far) * 16 + home_slot, 4095)
+    home_turn = jnp.where(home_k == 0, 0, zs // 2 - home_k)
+    home = jnp.where(code > 0, (2 * home_turn + home_far) * 16 + home_slot, 4095)
     home_cols = jnp.transpose(jnp.broadcast_to(home, square).astype(F32)).astype(I32)[:, 0:1]
     code_col = jnp.transpose(jnp.broadcast_to(code, square).astype(F32))[:, 0:1]
     block_col = block_cols[:, 0:1]
@@ -340,10 +345,7 @@
     )
     signs = jnp.transpose(signs).astype(BF16)
     fi = iota((zs, 128), 0)
-    f_near = fi // 2
-    f_step = jnp.where(
-        fi % 2 == 0, f_near, jnp.where(f_near == 0, zs // 2, zs - f_near)
-    )
+    f_step = steps_of_flows(fi)
     pick = (f_step == iota((zs, 128), 1)).astype(F32).astype(BF16)
     rmeta2[...] = nn_dot(in_flow, codes) + nn_dot(pick, signs)
 
@@ -366,6 +368,8 @@
         return carry
 
     lax.fori_loop(1, zs, start_plan, 0)
+
+    lax.fori_loop(2, groups, dispatch_more, 0)
 
     rank = down.shape[0] // 2
     learn = rows.shape[0]
@@ -388,15 +392,12 @@
             dst_ref=lpart_got.at[j - 1],
             send_sem=lpart_send_sem,
             recv_sem=lpart_got_sem,
-            device_id=(me, (t + j) % ts),
+            device_id=(me, t_at[j]),
             device_id_type=MESH,
         )
 
-    def start_lpart(j, carry):
+    for j in range(1, ts):
         lpart_copy(j).start()
-        return carry
-
-    lax.fori_loop(1, ts, start_lpart, 0)
 
     def wait_group(g, ref, size, sems):
         @pl.when(g == 0)
@@ -429,7 +430,7 @@
             dst_ref=part_got.at[g, j - 1],
             send_sem=part_send_sem,
             recv_sem=part_got_sems.at[g],
-            device_id=(me, (t + j) % ts),
+            device_id=(me, t_at[j]),
             device_id_type=MESH,
         )
 
@@ -452,11 +453,8 @@
         two = two.reshape(2, pairs // 2, 8, 2 * rank)
         part[g] = jnp.where(left3[: pairs // 2], two[0], two[1])
 
-        def start(j, carry):
+        for j in range(1, ts):
             part_copy(g, j).start()
-            return carry
-
-        lax.fori_loop(1, ts, start, 0)
 
     def start_cross(g):
         for half in range(2):
@@ -506,10 +504,7 @@
         lane16 = iota((zs, 128), 1)
         source = (z + zs - f_step) % zs
         other_f = iota((zs, zs), 1)
-        other_near = other_f // 2
-        other_step = jnp.where(
-            other_f % 2 == 0, other_near, jnp.where(other_near == 0, zs // 2, zs - other_near)
-        )
+        other_step = steps_of_flows(other_f)
         other = (z + zs - other_step) % zs
         first = (other < source[:, 0:1]).astype(F32).astype(BF16)
         ahead = nn_dot(first, plan.astype(BF16))
@@ -581,7 +576,7 @@
             src_ref=asend.at[at],
             dst_ref=agot.at[at],
             send_sem=asend_sem,
-            recv_sem=agot_sems.at[f // 2],
+            recv_sem=agot_sems.at[lax.div(f, 2)],
             device_id=(z_peer(zs - flow_step(f)), t),
             device_id_type=MESH,
         )
@@ -630,25 +625,25 @@
             lax.fori_loop(2 * g, 2 * g + 2, start_a, 0)
 
     def stage(s, carry):
+        @pl.when(s == 2)
+        def _():
+            read_plans()
+
+        @pl.when(jnp.logical_and(s >= 2, s < groups + 2))
+        def _():
+            deltas(s - 2)
+
+        @pl.when(s >= 3)
+        def _():
+            relay(s - 3)
+
         @pl.when(s < groups)
         def _():
             ranks(s)
 
-        @pl.when(s == 1)
-        def _():
-            read_plans()
-
-        @pl.when(jnp.logical_and(s >= 1, s < groups + 1))
-        def _():
-            deltas(s - 1)
-
-        @pl.when(s >= 2)
-        def _():
-            relay(s - 2)
-
-        return carry
-
-    lax.fori_loop(0, groups + 2, stage, 0)
+        return carry
+
+    lax.fori_loop(0, groups + 3, stage, 0)
 
     spare = SPARE * CHUNKS
     fsend[...] = spill[...].astype(BF16)
@@ -691,7 +686,7 @@
             src_ref=bsend.at[at],
             dst_ref=bgot.at[at],
             send_sem=bsend_sem,
-            recv_sem=bgot_sems.at[f // 4],
+            recv_sem=bgot_sems.at[lax.div(f, 4)],
             device_id=(z_peer(zs - flow_step(f)), t),
             device_id_type=MESH,
         )
@@ -775,7 +770,7 @@
     worst = flagx_send[...]
     for dx in range(1, xs):
         worst = jnp.maximum(worst, flagx_got[dx - 1])
-    flag_out[...] = jnp.broadcast_to(worst, (8, 128))
+    flag_out[0] = jnp.max(worst).astype(I32)
 
     def drain(view, sem):
         pltpu.make_async_copy(view, view, sem).wait()
@@ -793,70 +788,385 @@
     drain(part_got, part_send_sem)
 
 
-def lookup(table, wanted):
-    hits = wanted[:, None] == jnp.arange(table.shape[0], dtype=jnp.int32)[None, :]
-    return jnp.sum(jnp.where(hits, table[None, :], 0), axis=1)
+def padded_kernel(
+    geometry,
+    dec_hbm,
+    dec_index_hbm,
+    store_hbm,
+    down_hbm,
+    up_hbm,
+    delta_out,
+    dec_index_ref,
+    store_ref,
+    dec,
+    down,
+    up,
+    send,
+    got,
+    meta2,
+    meta_send,
+    meta_got,
+    part,
+    part_got,
+    dsend,
+    dgot,
+    total,
+    load_sems,
+    send_sem,
+    got_sems,
+    meta_send_sem,
+    meta_got_sems,
+    part_send_sem,
+    part_got_sems,
+    dsend_sem,
+    dgot_sems,
+):
+    zs, xs, ts, shrink, expand = geometry
+    owners = zs * xs
+    wide = 2 * xs
+    groups = zs // 2
+    gr = wide * BLOCK
+    me = lax.axis_index("dp")
+    t = lax.axis_index("tensor")
+    z, x = me // xs, me % xs
+    count = dec.shape[0]
+    wc = dec.shape[1] // CHUNKS
+    hc = up.shape[1] // CHUNKS
+
+    def offset(i):
+        k = (zs // 2 - i // wide) % (zs // 2)
+        half = (i % wide) // xs
+        dz = k + half * (zs - 2 * k - (zs // 2) * ((zs - k) // zs))
+        return dz, i % xs
+
+    def owner_of(i):
+        dz, dx = offset(i)
+        return ((z + dz) % zs) * xs + (x + dx) % xs
+
+    def source_of(i):
+        dz, dx = offset(i)
+        return ((z + zs - dz) % zs) * xs + (x + xs - dx) % xs
+
+    def load(k, src, dst):
+        return pltpu.make_async_copy(src, dst, load_sems.at[k])
+
+    loads = [
+        load(0, dec_hbm, dec),
+        load(1, dec_index_hbm, dec_index_ref),
+        load(2, store_hbm, store_ref),
+        load(3, down_hbm, down),
+        load(4, up_hbm, up),
+    ]
+    for one in loads:
+        one.start()
+
+    barrier = pltpu.get_barrier_semaphore()
+
+    def greet(i, carry):
+        pl.semaphore_signal(barrier, inc=1, device_id=(owner_of(i), t), device_id_type=MESH)
+        return carry
+
+    lax.fori_loop(1, owners, greet, 0)
+
+    def greet_t(j, carry):
+        pl.semaphore_signal(barrier, inc=1, device_id=(me, (t + j) % ts), device_id_type=MESH)
+        return carry
+
+    lax.fori_loop(1, ts, greet_t, 0)
+
+    for one in loads[1:3]:
+        one.wait()
+
+    adapters = store_ref.shape[1]
+    hits = (iota((adapters, count), 0) == dec_index_ref[...]).astype(F32).astype(BF16)
+    table = jnp.broadcast_to(store_ref[...], (8, adapters)).astype(F32).astype(BF16)
+    slot = nn_dot(table, hits)[0:1].astype(I32)
+    owner, local = slot // 2, slot % 2
+    dz = (owner // xs - z + zs) % zs
+    dx = (owner % xs - x + xs) % xs
+    half = (dz >= zs // 2).astype(I32)
+    k = jnp.where(dz < zs // 2, dz, jnp.where(dz == zs // 2, 0, zs - dz))
+    turn = jnp.where(k == 0, 0, zs // 2 - k)
+    block = turn * wide + half * xs + dx
+    square = (count, count)
+    block_rows = jnp.broadcast_to(block, square)
+    block_cols = jnp.transpose(block_rows.astype(F32)).astype(I32)
+    same = jnp.logical_and(block_rows == block_cols, iota(square, 0) < iota(square, 1))
+    before = jnp.sum(same.astype(F32), axis=0, keepdims=True).astype(I32)
+    place = block * BLOCK + before
+    code = jnp.broadcast_to(place * 2 + local, square)
+    code_cols = jnp.transpose(code.astype(F32)).astype(I32)
+    place_cols = code_cols // 2
+    named = (code_cols % 2 + 1).astype(F32)
+    lanes = iota((count, 128), 1)
+    slot_cols = jnp.broadcast_to(place_cols[:, 0:1] % BLOCK, (count, 128))
+    spread = jnp.where(
+        lanes % DEPTH == slot_cols, jnp.broadcast_to(named[:, 0:1], (count, 128)), 0.0
+    )
+    in_block = (iota((owners, count), 0) == block).astype(F32).astype(BF16)
+    meta2[...] = nn_dot(in_block, spread.astype(BF16))
+
+    def lift(i, carry):
+        meta_send[i] = meta2[pl.ds(i, 1), :]
+        return carry
+
+    lax.fori_loop(0, owners, lift, 0)
+    meta_got[0] = meta2[0:1, :]
+
+    loads[0].wait()
+    pl.semaphore_wait(barrier, owners - 1 + ts - 1)
+
+    def row_copy(i):
+        at = pl.ds(pl.multiple_of(i * BLOCK, BLOCK), BLOCK)
+        return pltpu.make_async_remote_copy(
+            src_ref=send.at[at],
+            dst_ref=got.at[at],
+            send_sem=send_sem,
+            recv_sem=got_sems.at[i // wide],
+            device_id=(owner_of(i), t),
+            device_id_type=MESH,
+        )
+
+    def meta_copy(i):
+        return pltpu.make_async_remote_copy(
+            src_ref=meta_send.at[i],
+            dst_ref=meta_got.at[i],
+            send_sem=meta_send_sem,
+            recv_sem=meta_got_sems.at[i // wide],
+            device_id=(owner_of(i), t),
+            device_id_type=MESH,
+        )
+
+    def start_rows(i, carry):
+        meta_copy(i).start()
+        row_copy(i).start()
+        return carry
+
+    def dispatch(g):
+        base = pl.multiple_of(g * gr, gr)
+        rel = iota((gr, count), 0) + base
+        sum_rows = jnp.zeros((gr, wc), F32)
+        for c in range(CHUNKS):
+            chosen = (rel == place + c * DEPTH).astype(F32).astype(BF16)
+            sum_rows += nn_dot(chosen, dec[:, c * wc : (c + 1) * wc])
+        send[pl.ds(base, gr), :] = sum_rows.astype(BF16)
+
+    dispatch(0)
+    lax.fori_loop(1, wide, start_rows, 0)
+    got[0:BLOCK, :] = send[0:BLOCK, :]
+
+    def dispatch_more(g, carry):
+        dispatch(g)
+        lax.fori_loop(g * wide, (g + 1) * wide, start_rows, 0)
+        return carry
+
+    lax.fori_loop(1, groups, dispatch_more, 0)
+
+    rank = down.shape[0] // 2
+    loads[3].wait()
+    loads[4].wait()
+
+    def wait_group(g, ref, size, sems):
+        @pl.when(g == 0)
+        def _():
+            view = ref.at[pl.ds(size, (wide - 1) * size)]
+            pltpu.make_async_copy(view, view, sems.at[g]).wait()
+
+        @pl.when(g > 0)
+        def _():
+            view = ref.at[pl.ds(pl.multiple_of(g * wide * size, wide * size), wide * size)]
+            pltpu.make_async_copy(view, view, sems.at[g]).wait()
+
+    chunk_of = (iota((gr, 2 * rank), 0) % BLOCK) // DEPTH
+    lane = iota((gr, 2 * rank), 1)
+
+    def chosen_mask(g):
+        ids = meta_got[pl.ds(g * wide, wide)]
+        ids = jnp.broadcast_to(ids, (wide, BLOCK, 128)).reshape(gr, 128)
+        mine = iota((gr, 128), 1) == iota((gr, 128), 0) % DEPTH
+        which = jnp.sum(jnp.where(mine, ids, 0.0), axis=1, keepdims=True)
+        return (which == (lane // rank + 1).astype(F32)).astype(F32)
+
+    pairs = wide // 2
+    top3 = iota((wide, 8, 2 * rank), 1) < DEPTH
+    left3 = iota((wide, 8, 2 * rank), 2) < rank
+
+    def part_copy(g, j):
+        return pltpu.make_async_remote_copy(
+            src_ref=part.at[g],
+            dst_ref=part_got.at[g, j - 1],
+            send_sem=part_send_sem,
+            recv_sem=part_got_sems.at[g],
+            device_id=(me, (t + j) % ts),
+            device_id_type=MESH,
+        )
+
+    def ranks(g):
+        wait_group(g, got, BLOCK, got_sems)
+        wait_group(g, meta_got, 1, meta_got_sems)
+        at = pl.ds(pl.multiple_of(g * gr, gr), gr)
+        block_rows = got[at, :]
+        both = jnp.zeros((gr, 2 * rank), F32)
+        for c in range(CHUNKS):
+            one = nt_dot(block_rows, down[:, c * wc : (c + 1) * wc])
+            both = both + jnp.where(chunk_of == c, one, 0.0)
+        both = both * chosen_mask(g)
+        both = both.reshape(wide, 2, 8, 2 * rank)
+        both = both[:, 0] + both[:, 1]
+        both = both + pltpu.roll(both, DEPTH, 1)
+        both = both + pltpu.roll(both, rank, 2)
+        both = both.reshape(2, pairs, 8, 2 * rank)
+        two = jnp.where(top3[:pairs], both[0], both[1])
+        two = two.reshape(2, pairs // 2, 8, 2 * rank)
+        part[g] = jnp.where(left3[: pairs // 2], two[0], two[1])
+
+        def start(j, carry):
+            part_copy(g, j).start()
+            return carry
+
+        lax.fori_loop(1, ts, start, 0)
+
+    def delta_copy(i):
+        at = pl.ds(pl.multiple_of(i * BLOCK, BLOCK), BLOCK)
+        return pltpu.make_async_remote_copy(
+            src_ref=dsend.at[at],
+            dst_ref=dgot.at[at],
+            send_sem=dsend_sem,
+            recv_sem=dgot_sems.at[i // wide],
+            device_id=(source_of(i), t),
+            device_id_type=MESH,
+        )
+
+    def start_delta(i, carry):
+        delta_copy(i).start()
+        return carry
+
+    def deltas(g):
+        view = part_got.at[g]
+        pltpu.make_async_copy(view, view, part_got_sems.at[g]).wait()
+        v = part[g]
+        for j in range(ts - 1):
+            v = v + part_got[g, j]
+        v = (v * shrink).astype(BF16).astype(F32)
+        turned = pltpu.roll(v, rank, 2)
+        keep = left3[: pairs // 2]
+        two = jnp.concatenate([jnp.where(keep, v, turned), jnp.where(keep, turned, v)], axis=0)
+        turned = pltpu.roll(two, DEPTH, 1)
+        keep = top3[:pairs]
+        both = jnp.concatenate([jnp.where(keep, two, turned), jnp.where(keep, turned, two)], axis=0)
+        both = jnp.broadcast_to(both[:, None], (wide, 2, 8, 2 * rank)).reshape(gr, 2 * rank)
+        both = both * chosen_mask(g)
+        base = pl.multiple_of(g * gr, gr)
+        sum_rows = jnp.zeros((gr, hc), F32)
+        for c in range(CHUNKS):
+            left = jnp.where(chunk_of == c, both, 0.0).astype(BF16)
+            sum_rows += nn_dot(left, up[:, c * hc : (c + 1) * hc])
+        dsend[pl.ds(base, gr), :] = (sum_rows * expand).astype(BF16)
+
+        @pl.when(g == 0)
+        def _():
+            dgot[0:BLOCK, :] = dsend[0:BLOCK, :]
+            lax.fori_loop(1, wide, start_delta, 0)
+
+        @pl.when(g > 0)
+        def _():
+            lax.fori_loop(g * wide, (g + 1) * wide, start_delta, 0)
+
+    ranks(0)
+
+    def step(g, carry):
+        ranks(g)
+        deltas(g - 1)
+        return carry
+
+    lax.fori_loop(1, groups, step, 0)
+    deltas(groups - 1)
+
+    total[...] = jnp.zeros_like(total)
+    place_128 = jnp.broadcast_to(place_cols[:, 0:1], (count, gr))
+
+    def combine(g, carry):
+        wait_group(g, dgot, BLOCK, dgot_sems)
+        base = pl.multiple_of(g * gr, gr)
+        rel = iota((count, gr), 1) + base
+        arrived = dgot[pl.ds(base, gr), :]
+        for c in range(CHUNKS):
+            chosen = (rel == place_128 + c * DEPTH).astype(F32).astype(BF16)
+            total[:, c * hc : (c + 1) * hc] += nn_dot(chosen, arrived)
+        return carry
+
+    lax.fori_loop(0, groups, combine, 0)
+    delta_out[...] = total[...].astype(BF16)
+
+    def drain(view, sem):
+        pltpu.make_async_copy(view, view, sem).wait()
+
+    drain(send.at[pl.ds(BLOCK, (owners - 1) * BLOCK)], send_sem)
+    drain(meta_send.at[pl.ds(1, owners - 1)], meta_send_sem)
+    drain(dsend.at[pl.ds(BLOCK, (owners - 1) * BLOCK)], dsend_sem)
+    drain(part_got, part_send_sem)
 
 
 def padded_exchange(
     decode_input_rows,
     decode_adapter_index,
     adapter_storage_index,
-    adapter_down_weight,
-    adapter_up_weight,
+    down_rows,
+    up_rows,
 ):
     owners = lax.axis_size("dp")
-    split_points = lax.axis_size("tensor")
-    holder_mask, rank_extent, width_portion = adapter_down_weight.shape
-    hidden_portion = adapter_up_weight.shape[2]
-    shrink = (width_portion * split_points) ** (-0.5)
-    expand = rank_extent ** (-0.5)
-    row_count = decode_input_rows.shape[0]
-    slot_depth = 2 * row_count // owners
-    total_slots = owners * slot_depth
-    slot_row = lookup(adapter_storage_index, decode_adapter_index)
-    target = slot_row // holder_mask
-    local_slot = slot_row % holder_mask
-    target_hot = (target[:, None] == jnp.arange(owners, dtype=jnp.int32)[None, :]).astype(jnp.int32)
-    before = jnp.cumsum(target_hot, axis=0) - target_hot
-    position = target * slot_depth + jnp.sum(before * target_hot, axis=1)
-    matches = jnp.arange(total_slots, dtype=jnp.int32)[:, None] == position[None, :]
-    dispatch = matches.astype(jnp.bfloat16)
-    send_rows = jnp.dot(dispatch, decode_input_rows, preferred_element_type=jnp.float32).astype(
-        jnp.bfloat16
+    ts = lax.axis_size("tensor")
+    xs = 4
+    zs = owners // xs
+    count, width = decode_input_rows.shape
+    both, hidden = up_rows.shape
+    groups = zs // 2
+    wide = 2 * xs
+    hbm = pl.BlockSpec(memory_space=pltpu.HBM)
+    dma = pltpu.SemaphoreType.DMA
+    packed = (wide // 4, 8, both)
+    geometry = (zs, xs, ts, (width * ts) ** (-0.5), (both // 2) ** (-0.5))
+    return pl.pallas_call(
+        functools.partial(padded_kernel, geometry),
+        out_shape=jax.ShapeDtypeStruct((count, hidden), BF16),
+        in_specs=[hbm] * 5,
+        out_specs=pl.BlockSpec(memory_space=pltpu.VMEM),
+        scratch_shapes=[
+            pltpu.VMEM((1, count), I32),
+            pltpu.VMEM((1, adapter_storage_index.shape[0]), I32),
+            pltpu.VMEM((count, width), BF16),
+            pltpu.VMEM((both, width), BF16),
+            pltpu.VMEM((both, hidden), BF16),
+            pltpu.VMEM((owners * BLOCK, width // CHUNKS), BF16),
+            pltpu.VMEM((owners * BLOCK, width // CHUNKS), BF16),
+            pltpu.VMEM((owners, 128), F32),
+            pltpu.VMEM((owners, 1, 128), F32),
+            pltpu.VMEM((owners, 1, 128), F32),
+            pltpu.VMEM((groups,) + packed, F32),
+            pltpu.VMEM((groups, ts - 1) + packed, F32),
+            pltpu.VMEM((owners * BLOCK, hidden // CHUNKS), BF16),
+            pltpu.VMEM((owners * BLOCK, hidden // CHUNKS), BF16),
+            pltpu.VMEM((count, hidden), F32),
+            dma((5,)),
+            dma,
+            dma((groups,)),
+            dma,
+            dma((groups,)),
+            dma,
+            dma((groups,)),
+            dma,
+            dma((groups,)),
+        ],
+        compiler_params=pltpu.CompilerParams(
+            collective_id=1, has_side_effects=True, vmem_limit_bytes=VMEM_LIMIT
+        ),
+    )(
+        decode_input_rows,
+        decode_adapter_index.reshape(1, count),
+        adapter_storage_index.reshape(1, -1),
+        down_rows,
+        up_rows,
     )
-    filled = jnp.any(matches, axis=1)
-    send_local = jnp.where(filled, jnp.sum(jnp.where(matches, local_slot[None, :], 0), axis=1), -1)
-    send_rows = send_rows.reshape(owners, slot_depth, width_portion)
-    send_local = send_local.astype(jnp.bfloat16).reshape(owners, slot_depth)
-    flattened_second = adapter_up_weight.reshape(holder_mask * rank_extent, hidden_portion)
-    got_rows, got_local = (
-        lax.all_to_all(send_rows, "dp", split_axis=0, concat_axis=0, tiled=True),
-        lax.all_to_all(send_local, "dp", split_axis=0, concat_axis=0, tiled=True),
-    )
-    sources, items = got_local.shape
-    flattened_rows = got_rows.reshape(sources * items, width_portion)
-    which_slot = got_local.reshape(-1).astype(jnp.float32)
-    chosen = (which_slot[:, None] == jnp.arange(holder_mask, dtype=jnp.float32)[None, :]).astype(
-        jnp.float32
-    )
-    partial_output = jnp.einsum(
-        "lm,kjm->lkj", flattened_rows, adapter_down_weight, preferred_element_type=jnp.float32
-    )
-    to_sum = partial_output.reshape(sources * items, holder_mask * rank_extent)
-    summed = lax.psum(to_sum, "tensor")
-    spread = summed.reshape(sources * items, holder_mask, rank_extent) * chosen[:, :, None]
-    hidden = (
-        (spread * shrink).reshape(sources * items, holder_mask * rank_extent).astype(jnp.bfloat16)
-    )
-    delta_rows = jnp.dot(hidden, flattened_second, preferred_element_type=jnp.float32) * expand
-    answer = delta_rows.astype(jnp.bfloat16).reshape(sources, items, hidden_portion)
-    returned = lax.all_to_all(answer, "dp", split_axis=0, concat_axis=0, tiled=True)
-    merged = returned.reshape(total_slots, hidden_portion)
-    dec_delta = jnp.einsum(
-        "mr,mf->rf", dispatch, merged, preferred_element_type=jnp.float32
-    ).astype(jnp.bfloat16)
-    return dec_delta
 
 
 def local(
@@ -894,10 +1204,10 @@
             jax.ShapeDtypeStruct((count, hidden), BF16),
             jax.ShapeDtypeStruct((held * rank, width), BF16),
             jax.ShapeDtypeStruct((held * rank, hidden), BF16),
-            jax.ShapeDtypeStruct((8, 128), F32),
+            jax.ShapeDtypeStruct((1,), I32),
         ),
         in_specs=[hbm] * 10,
-        out_specs=(vmem, vmem, vmem, vmem),
+        out_specs=(vmem, vmem, vmem, pl.BlockSpec(memory_space=pltpu.SMEM)),
         scratch_shapes=[
             pltpu.VMEM((1, count), I32),
             pltpu.VMEM((1, adapter_storage_index.shape[0]), I32),
@@ -961,7 +1271,7 @@
             dma((4,)),
         ],
         compiler_params=pltpu.CompilerParams(
-            collective_id=0, has_side_effects=True, vmem_limit_bytes=58 * 1024 * 1024
+            collective_id=0, has_side_effects=True, vmem_limit_bytes=VMEM_LIMIT
         ),
     )(
         decode_adapter_index.reshape(1, count),
@@ -980,11 +1290,11 @@
             decode_input_rows,
             decode_adapter_index,
             adapter_storage_index,
-            adapter_down_weight,
-            adapter_up_weight,
+            adapter_down_weight.reshape(held * rank, width),
+            adapter_up_weight.reshape(held * rank, hidden),
         )
 
-    delta = lax.cond(flag[0, 0] > 0.5, padded, lambda: delta)
+    delta = lax.cond(flag[0] > 0, padded, lambda: delta)
     return delta, down.reshape(held, rank, width), up.reshape(held, rank, hidden)
 
 

time: 160 us -> 125 us (0.78)
  Pallas kernels: 136 us -> 118 us
  between operations: 16.2 us -> 2.62 us
  local copies, waits for them, and re-layouts: 5.15 us -> 3.51 us
    pallas_call x1, Pallas kernels: 136 us -> 118 us  [local(): pl.pallas_call(functools.partial(kernel, (zs, xs, ts, shrink, expand)), o...]
where the time goes in v4:
time: 125 us; the launch traced here: 124 us
  Pallas kernels  118 us (94%)
  local copies, waits for them, and re-layouts  3.51 us (3%)
  between operations  2.62 us (2%)
    pallas_call x1, Pallas kernels, local(): pl.pallas_call(functools.partial(kernel, (zs, xs, ts, shrink, expand)), o...  118 us
    unnamed x17, local copies, waits for them, and re-layouts  3.51 us

profile of v4, /device:TPU:24, one launch (start us, length us, event | category | flops | bytes accessed | tf_op | source)
XLA Modules:
  0.0 123.9 jit_solution(8338500998161278421)
XLA Ops:
  1.9 0.0 copy-start.5
  1.9 0.0 copy-start.6
  1.9 0.6 copy-done.5
  2.6 0.0 copy-done.6
  2.6 0.0 copy-start
  2.6 0.0 copy-start.1
  2.6 0.0 copy-start.2
  2.6 117.8 %shard_map.112 = (bf16[128,3584]{1,0:T(8,128)(2,1)S(1)}, bf16[128,1536]{1,0:T(8,128)(2,1)}, bf16[128,3584]{1,0:T(8,128)(2,1)}, s32[1]{0:T(128)}) custom-call(s32[1,128]{1,0:T(1,128)S(1)} %bitcast.19, s32[1,128]{1,0:T(1,128)S(1)} %bitcast.17, s32[128]{0:T(128)S(1)} %copy-done.5, s32[1]{0:T(128)S(6)} %copy.17.blk_hbm, s32[1]{0:T(128)S(6)} %copy.18.live_hbm, ...), custom_call_target="tpu_custom_call" | custom-call | tf_op jit(solution)/shard_map/pallas_call | solution.py:1201
  121.0 0.0 copy-done
  121.0 0.0 copy-done.1
  121.0 0.0 copy-done.2
  121.1 0.0 copy-start.4
  121.1 0.0 copy-start.3
  121.1 0.9 copy.19
  122.0 0.2 copy-done.4
  122.3 0.7 copy.20
  123.0 0.0 copy-done.3
  123.0 0.9 copy.21
  (1 shorter events, 0.0 us)
Async XLA Ops:
  1.9 0.7 copy-start.5
  1.9 0.7 copy-start.6
  2.6 118.4 %copy-start = (bf16[2,64,3584]{2,1,0:T(8,128)(2,1)S(1)}, bf16[2,64,3584]{2,1,0:T(8,128)(2,1)}, u32[]{:S(2)}) copy-start(bf16[2,64,3584]{2,1,0:T(8,128)(2,1)} %param.19) | copy-start | bytes 2752516
  2.6 118.4 %copy-start.1 = (bf16[128,1536]{1,0:T(8,128)(2,1)S(1)}, bf16[128,1536]{1,0:T(8,128)(2,1)}, u32[]{:S(2)}) copy-start(bf16[128,1536]{1,0:T(8,128)(2,1)} %dec_hbm.1) | copy-start | bytes 1179652
  2.6 118.4 %copy-start.2 = (bf16[2,64,1536]{2,1,0:T(8,128)(2,1)S(1)}, bf16[2,64,1536]{2,1,0:T(8,128)(2,1)}, u32[]{:S(2)}) copy-start(bf16[2,64,1536]{2,1,0:T(8,128)(2,1)} %param.18) | copy-start | bytes 1179652
  121.1 1.2 copy-start.4
  121.1 1.9 %copy-start.3 = (bf16[128,3584]{1,0:T(8,128)(2,1)S(1)}, bf16[128,3584]{1,0:T(8,128)(2,1)}, u32[]{:S(2)}) copy-start(bf16[128,3584]{1,0:T(8,128)(2,1)} %get-tuple-element.29) | copy-start | bytes 2752516
